TPU v7x, 512 devices: a whole 4x8x8 slice. The times are simulated.
512 devices in a mesh: grid: 128 (over z, y, x_hi), chan: 4 (over x_lo, core).
Axes of the slice: x: 4 (x_hi: 2, x_lo: 2; x = x_hi * 2 + x_lo), y: 8, z: 8, core: 2. Of those that a mesh axis runs over, the one named last changes fastest.
Arguments:
- field: bfloat16 [16, 1024, 768], P(None, 'grid', 'chan'), may hold values from -6 to 6
- cotangent: bfloat16 [16, 1024, 768], P(None, 'grid', 'chan'), may hold values from -8.4 to 8.4
- pre_hidden: bfloat16 [16, 1024, 3072], P(None, 'grid', 'chan'), may hold values from -6 to 6
- w_up: bfloat16 [768, 3072], P(None, 'chan'), may hold values from -0.21875 to 0.21875
- w_down: bfloat16 [3072, 768], P('chan'), may hold values from -0.109375 to 0.109375
- gain: float32 [768], P('chan'), may hold values from 0.25 to 1.75
- tap_weights: float32 [20, 768], P(None, 'chan'), may hold values from -12 to 12
- basis: float32 [16, 20], replicated, may hold values from 0.05 to 0.5
- lon_offsets: int32 [16, 20], replicated, may hold values from -8 to 8, as said below
Outputs:
- field_grad: bfloat16 [16, 1024, 768], P(None, 'grid', 'chan')
- gain_grad: float32 [768], P('chan')
- tap_grad: float32 [20, 768], P(None, 'chan')
Inputs may be any that keep to these rules, and one draw needn't show every extreme that they name: `lon_offsets`: both ends of the range are reached in every draw.
All inputs are finite; a program needn't handle non-finite values.
Results may differ from a plain program's by a relative error of at most 0.005.
Values may be sent and summed in bfloat16 or wider, within the bound.
No kernel may reach another device: no remote copies, remote signals or barrier semaphores. Data moves between devices by JAX's collectives and lax.ppermute only.
A program may use at most 64 MiB of HBM per device.

v0:
```python
import math

import jax
import jax.numpy as jnp
from jax import lax
from jax.sharding import PartitionSpec as P

D = 768
HALO = 8
REACH = 2
PER_ROW = 4


EPSILON = 1e-05
INV_SQRT_TWO = 0.7071067811865476
INV_SQRT_TWO_PI = 0.3989422804014327


def extended(value, sides, width):
    for axis, dim in sides:
        size, length = (lax.axis_size(axis), value.shape[dim])
        up = [(i, (i + 1) % size) for i in range(size)]
        down = [(j, i) for i, j in up]
        last = lax.slice_in_dim(value, length - width, length, axis=dim)
        leading = lax.slice_in_dim(value, 0, width, axis=dim)
        before = lax.ppermute(last, axis, up)
        after = lax.ppermute(leading, axis, down)
        value = jnp.concatenate([before, value, after], axis=dim)
    return value


def window_rows(source, row_start, col_start, span):
    chan_depth = source.shape[2]

    def single(row_at, col_at):
        return lax.dynamic_slice(source, (row_at, col_at, 0), (1, span, chan_depth))[0]

    return jax.vmap(jax.vmap(single))(row_start, col_start)


def per_device(field, cotangent, pre_hidden, w_up, w_down, gain, tap_weights, basis, lon_offsets):
    row_count, lon_count, chan_depth = field.shape
    tap_count = basis.shape[1]
    hidden_dev = pre_hidden.shape[2]
    cell_count = row_count * lon_count
    tap_ids = jnp.arange(tap_count, dtype=jnp.int32)
    row_shift = tap_ids // PER_ROW
    row_ids = jnp.arange(row_count, dtype=jnp.int32)
    weight_tap = basis[:, :, None] * tap_weights[None, :, :]
    scale_sum = 1.0 / math.sqrt(row_count * lon_count * lax.axis_size("grid"))
    field_rim = extended(field, (("grid", 1),), HALO)
    field_rows = jnp.pad(field_rim, ((REACH, REACH), (0, 0), (0, 0)))
    field_win = window_rows(
        field_rows, row_ids[:, None] + row_shift[None, :], HALO + lon_offsets, lon_count
    )
    forward = jnp.sum(weight_tap[:, :, None, :] * field_win, axis=1)
    squares = jnp.sum(forward * forward, axis=2)
    square_total = lax.psum(squares, "chan")
    flat_cot = cotangent.reshape(cell_count, chan_depth)
    hidden_grad = lax.dot_general(
        lax.all_gather(flat_cot, "chan", axis=1, tiled=True),
        w_down,
        (((1,), (1,)), ((), ())),
        preferred_element_type=jnp.float32,
    )
    pre_value = pre_hidden.reshape(cell_count, hidden_dev).astype(jnp.float32)
    slope = (
        0.5 * (1.0 + lax.erf(pre_value * INV_SQRT_TWO))
        + pre_value * jnp.exp(-0.5 * pre_value * pre_value) * INV_SQRT_TWO_PI
    )
    pre_grad = (hidden_grad * slope).astype(jnp.bfloat16)
    norm_grad = lax.psum_scatter(
        lax.dot_general(
            w_up, pre_grad, (((1,), (1,)), ((), ())), preferred_element_type=jnp.float32
        ),
        "chan",
        scatter_dimension=0,
        tiled=True,
    ).T.reshape(row_count, lon_count, chan_depth)
    scaled = gain * norm_grad
    products = jnp.sum(forward * scaled, axis=2)
    product_total = lax.psum(products, "chan")
    inv_rms = lax.rsqrt(square_total / D + EPSILON)
    field_term = inv_rms[..., None] * scaled - forward * (inv_rms**3 * product_total / D)[..., None]
    gain_local = jnp.sum(norm_grad * forward * inv_rms[..., None], axis=(0, 1)) * scale_sum
    tap_inner = jnp.sum(field_term[:, None] * field_win, axis=2)
    tap_local = (
        jnp.einsum("rk,rkc->kc", basis, tap_inner, precision=lax.Precision.HIGHEST) * scale_sum
    )
    gain_grad, tap_grad = lax.psum((gain_local, tap_local), "grid")
    grad_rim = extended(field_term, (("grid", 1),), HALO)
    grad_rows = jnp.pad(grad_rim, ((REACH, REACH), (0, 0), (0, 0)))
    source_rows = row_ids[:, None] + 2 * REACH - row_shift[None, :]
    offsets_pad = jnp.pad(lon_offsets, ((REACH, REACH), (0, 0)))
    weight_pad = jnp.pad(weight_tap, ((REACH, REACH), (0, 0), (0, 0)))
    source_offsets = jnp.take_along_axis(offsets_pad, source_rows, axis=0)
    source_weight = weight_pad[source_rows, tap_ids[None, :]]
    grad_win = window_rows(grad_rows, source_rows, HALO - source_offsets, lon_count)
    adjoint = jnp.sum(source_weight[:, :, None, :] * grad_win, axis=1)
    field_grad = (cotangent.astype(jnp.float32) + adjoint).astype(jnp.bfloat16)
    return (field_grad, gain_grad, tap_grad)


def solution(mesh):
    placed = (
        P(None, "grid", "chan"),
        P(None, "grid", "chan"),
        P(None, "grid", "chan"),
        P(None, "chan"),
        P("chan", None),
        P("chan"),
        P(None, "chan"),
        P(),
        P(),
    )
    return jax.shard_map(
        per_device,
        mesh=mesh,
        in_specs=placed,
        out_specs=(P(None, "grid", "chan"), P("chan"), P(None, "chan")),
        check_vma=False,
    )
```

profile of v0, /device:TPU:2, one launch (start us, length us, event | category | flops | bytes accessed | tf_op | source)
XLA Modules:
  0.0 817.5 jit_solution(6316839325840320183)
XLA Ops:
  7.2 0.0 copy-start
  7.2 0.0 copy-start.3
  7.2 0.0 reduce-scatter.4.cloned.1.call-start
  7.2 0.9 copy.52
  8.2 15.4 %collective-permute-start.1 = (bf16[16,8,192]{2,0,1:T(8,128)(2,1)S(1)}, bf16[16,8,192]{2,0,1:T(8,128)(2,1)S(1)}, u32[]{:S(2)}, u32[]{:S(2)}) collective-permute-start(bf16[16,8,192]{2,0,1:T(8,128)(2,1)S(1)} %copy.52), channel_id=1, source_target_pairs={{4,0},{8,4},{12,8},{16,12},{20,16},{24,20},{28,24},{32,28},{36,32}... | collective-permute-start | bytes 147464 | tf_op jit(solution)/shard_map/ppermute | solution.py:27
  23.6 1.9 collective-permute-start
  25.5 0.9 copy.58
  26.5 5.6 all_gather.3
  32.1 0.0 copy-done
  32.1 2.2 convolution_bitcast_fusion
  34.3 0.9 copy.68
  35.2 0.0 reduce-scatter.4.cloned.1.call-update
  35.3 0.1 shift-left_or_fusion
  35.3 0.1 reshape.255
  35.4 0.0 copy-done.3
  35.4 0.0 copy-start.4
  35.5 0.0 copy-start.5
  35.5 2.6 gather_fusion.3
  38.1 0.1 gather.18
  38.2 0.0 copy-done.4
  38.2 0.0 copy-done.5
  38.2 0.1 broadcast_multiply_fusion
  38.3 0.1 shift-left_or_fusion.1
  38.4 0.1 copy.66
  38.5 0.1 reshape.235
  38.6 0.1 reshape.249
  38.7 0.1 reshape.242
  38.8 5.7 gather_fusion
  44.5 0.8 reshape.238
  45.3 0.0 collective-permute-done.1
  45.3 0.0 collective-permute-done
  45.3 0.1 fusion.16
  45.4 7.5 gather_fusion.1
  52.9 1.5 copy.55
  54.3 3.0 copy.56
  57.3 2.0 multiply_reduce_fusion.2
  59.4 0.1 multiply_reduce_fusion.3
  59.5 0.1 copy.70
  59.5 7.0 psum.28
  66.6 0.1 copy.63
  66.6 0.1 mul.182
  66.7 0.0 reduce-scatter.4.cloned.1.call-done
  66.8 1.0 copy.69
  67.7 0.0 copy-done.6
  67.8 0.1 fusion.25
  67.9 0.1 reduce_sum.62
  68.0 0.1 copy.60
  68.1 6.3 psum.29
  74.4 0.1 fusion.26
  74.5 0.1 copy.64
  74.6 8.4 %collective-permute-start.3 = (f32[16,8,192]{2,0,1:T(8,128)S(1)}, f32[16,8,192]{2,0,1:T(8,128)S(1)}, u32[]{:S(2)}, u32[]{:S(2)}) collective-permute-start(f32[16,8,192]{2,0,1:T(8,128)S(1)} %fusion.26), channel_id=1, source_target_pairs={{4,0},{8,4},{12,8},{16,12},{20,16},{24,20},{28,24},{32,28},{36,32}... | collective-permute-start | bytes 294920 | tf_op jit(solution)/shard_map/ppermute | solution.py:27
  83.0 1.9 collective-permute-start.2
  84.9 2.6 multiply_reduce_fusion
  87.5 0.4 fusion.10
  87.9 708.3 %all-reduce.4 = (f32[192]{0:T(256)}, f32[20,192]{1,0:T(8,128)}) all-reduce(f32[192]{0:T(256)S(1)} %broadcast_multiply_fusion.1, f32[20,192]{1,0:T(8,128)S(1)} %bitcast_multiply_fusion.3), channel_id=1, replica_groups=mesh['grid'=128,'chan'=4] {'grid'}, use_global_device_ids=true, to_apply=%region_8.9 | all-reduce | flops 4032 | bytes 32256 | tf_op jit(solution)/shard_map/psum | solution.py:90
  796.2 0.0 collective-permute-done.3
  796.2 0.0 collective-permute-done.2
  796.2 0.1 select_maximum_fusion
  796.3 9.5 %gather_fusion.2 = f32[320,8,192]{2,0,1:T(8,128)} fusion(f32[20,24,192]{2,0,1:T(8,128)S(1)} %select_maximum_fusion, s32[320]{0:T(512)S(1)} %reshape.249), kind=kCustom, calls=%fused_computation.2 | custom fusion | bytes 3936000 | tf_op jit(solution)/shard_map/vmap(vmap())/gather | solution.py:36
  805.8 3.3 copy.62
  809.1 0.0 copy-start.2
  809.1 0.3 multiply_reduce_fusion.1
  809.4 0.5 copy-done.2
  810.0 0.6 add_convert_fusion
  (11 shorter events, 0.1 us)
Async XLA Ops:
  7.2 24.9 %copy-start = (bf16[768,768]{1,0:T(8,128)(2,1)S(1)}, bf16[768,768]{1,0:T(8,128)(2,1)}, u32[]{:S(2)}) copy-start(bf16[768,768]{1,0:T(8,128)(2,1)} %param.12) | copy-start | bytes 3538948
  7.2 28.2 %copy-start.3 = (s32[16,20]{1,0:T(8,128)S(1)}, s32[16,20]{1,0:T(8,128)}, u32[]{:S(2)}) copy-start(s32[16,20]{1,0:T(8,128)} %param.17) | copy-start | bytes 3844
  7.2 59.6 %reduce-scatter.4.cloned.1.call-start = ((), (), s32[]{:S(2)}) async-start(), calls=%async_computation.1 | async-start | bytes 491520
  8.2 37.1 %collective-permute-start.1 = (bf16[16,8,192]{2,0,1:T(8,128)(2,1)S(1)}, bf16[16,8,192]{2,0,1:T(8,128)(2,1)S(1)}, u32[]{:S(2)}, u32[]{:S(2)}) collective-permute-start(bf16[16,8,192]{2,0,1:T(8,128)(2,1)S(1)} %copy.52), channel_id=1, source_target_pairs={{4,0},{8,4},{12,8},{16,12},{20,16},{24,20},{28,24},{32,28},{36,32}... | collective-permute-start | bytes 147464 | tf_op jit(solution)/shard_map/ppermute | solution.py:27
  23.6 21.7 %collective-permute-start = (bf16[16,8,192]{2,0,1:T(8,128)(2,1)S(1)}, bf16[16,8,192]{2,0,1:T(8,128)(2,1)S(1)}, u32[]{:S(2)}, u32[]{:S(2)}) collective-permute-start(bf16[16,8,192]{2,0,1:T(8,128)(2,1)S(1)} %copy.52), channel_id=1, source_target_pairs={{0,4},{4,8},{8,12},{12,16},{16,20},{20,24},{24,28},{28,32},{32,36}... | collective-permute-start | bytes 147464 | tf_op jit(solution)/shard_map/ppermute | solution.py:26
  35.4 2.7 copy-start.4
  35.5 2.7 copy-start.5
  57.3 10.4 %copy-start.6 = (f32[192]{0:T(256)S(1)}, f32[192]{0:T(256)}, u32[]{:S(2)}) copy-start(f32[192]{0:T(256)} %param.14) | copy-start | bytes 2308
  74.6 721.6 %collective-permute-start.3 = (f32[16,8,192]{2,0,1:T(8,128)S(1)}, f32[16,8,192]{2,0,1:T(8,128)S(1)}, u32[]{:S(2)}, u32[]{:S(2)}) collective-permute-start(f32[16,8,192]{2,0,1:T(8,128)S(1)} %fusion.26), channel_id=1, source_target_pairs={{4,0},{8,4},{12,8},{16,12},{20,16},{24,20},{28,24},{32,28},{36,32}... | collective-permute-start | bytes 294920 | tf_op jit(solution)/shard_map/ppermute | solution.py:27
  83.0 713.2 %collective-permute-start.2 = (f32[16,8,192]{2,0,1:T(8,128)S(1)}, f32[16,8,192]{2,0,1:T(8,128)S(1)}, u32[]{:S(2)}, u32[]{:S(2)}) collective-permute-start(f32[16,8,192]{2,0,1:T(8,128)S(1)} %fusion.26), channel_id=1, source_target_pairs={{0,4},{4,8},{8,12},{12,16},{16,20},{20,24},{24,28},{28,32},{32,36}... | collective-permute-start | bytes 294920 | tf_op jit(solution)/shard_map/ppermute | solution.py:26
  805.8 3.3 copy-start.1
  809.1 0.8 copy-start.2
Sparse Core Ops, SparseCore 0:
  35.4 18.1 reduce-scatter.3
where the time goes:
time: 818 us; the launch traced here: 817 us
  blocking collectives  727 us (89%)
  local copies, waits for them, and re-layouts  39.2 us (5%)
  starting transfers between devices  27.7 us (3%)
  between operations  14.3 us (2%)
    psum x1, blocking collectives, per_device(): gain_grad, tap_grad = lax.psum((gain_local, tap_local), 'grid')  708 us
    ppermute x2, starting transfers between devices, extended(): after = lax.ppermute(leading, axis, down)  23.8 us
    gather x4, local copies, waits for them, and re-layouts, single(): lax.dynamic_slice(source, (row_at, col_at, 0), (1, span, chan_depth))[0]  21.8 us
  transfers between devices with their start and end apart: 5, of which 0 were waited for; matrix products, arithmetic and copies ran while one was open for 4% of the time, Pallas kernels for 0%

commit v1 on v0

v1 whole, which is shorter than its diff:
```python
import math

import jax
import jax.numpy as jnp
from jax import lax
from jax.experimental import pallas as pl
from jax.experimental.pallas import tpu as pltpu
from jax.sharding import Mesh
from jax.sharding import PartitionSpec as P

ROWS = 16
LON = 8
CELLS = ROWS * LON
D = 768
CH = 192
HID = 768
TAPS = 20
REACH = 2
PER_ROW = 4
NCHAN = 4
EXT = 3 * LON
GRID = ("z", "y", "xh")

EPSILON = 1e-05
INV_SQRT_TWO = 0.7071067811865476
INV_SQRT_TWO_PI = 0.3989422804014327
SCALE = 1.0 / math.sqrt(16384.0)

F32 = jnp.float32
BF16 = jnp.bfloat16
NT = (((1,), (1,)), ((), ()))

SEND = 5 * CELLS + 16
PACK = 32
HALF = 11


def params():
    return pltpu.CompilerParams(vmem_limit_bytes=24 * 1024 * 1024)


VMEM = pl.BlockSpec(memory_space=pltpu.VMEM)
SMEM = pl.BlockSpec(memory_space=pltpu.SMEM)


def taps_from(row):
    out = []
    for k in range(TAPS):
        src = row + k // PER_ROW - REACH
        if 0 <= src < ROWS:
            out.append((k, src))
    return out


def fill_ext(ext, left, own, right):
    ext[1] = jnp.zeros((ROWS * EXT, 128), F32)
    for at, ref in enumerate((left, own, right)):
        v = ref[...].astype(F32)
        for r in range(ROWS):
            to = pl.ds(EXT * r + LON * at, LON)
            ext[0, to, :] = v[LON * r : LON * r + LON, :128]
            ext[1, to, : CH - 128] = v[LON * r : LON * r + LON, 128:]


def mlp_kernel(cot, pre, w_down, w_up, out, cot_all):
    for i in range(NCHAN):
        cot_all[:, CH * i : CH * (i + 1)] = cot[i]
    hidden = lax.dot_general(cot_all[...], w_down[...], NT, preferred_element_type=F32)
    v = pre[...].astype(F32)
    slope = (
        0.5 * (1.0 + lax.erf(v * INV_SQRT_TWO))
        + v * jnp.exp(-0.5 * v * v) * INV_SQRT_TWO_PI
    )
    grad = (hidden * slope).astype(BF16)
    for i in range(NCHAN):
        part = lax.dot_general(
            grad, w_up[CH * i : CH * (i + 1), :], NT, preferred_element_type=F32
        )
        out[CELLS * i : CELLS * (i + 1), :] = part.astype(BF16)


def forward_kernel(offs, basis, left, own, right, taps, gain, part, fwd, send, ext):
    fill_ext(ext, left, own, right)
    for r in range(ROWS):
        lo = jnp.zeros((LON, 128), F32)
        hi = jnp.zeros((LON, 128), F32)
        for k, src in taps_from(r):
            at = pl.ds(EXT * src + LON + offs[r, k], LON)
            lo += basis[r, k] * (taps[k : k + 1, :128] * ext[0, at, :])
            hi += basis[r, k] * (taps[k : k + 1, 128:] * ext[1, at, :])
        fwd[LON * r : LON * (r + 1), :128] = lo
        fwd[LON * r : LON * (r + 1), 128:] = hi[:, : CH - 128]
    send[: 4 * CELLS, :] = part[...]
    send[4 * CELLS : 5 * CELLS, :] = fwd[...].astype(BF16)
    g = gain[...]
    top = g.astype(BF16)
    mid = (g - top.astype(F32)).astype(BF16)
    low = (g - top.astype(F32) - mid.astype(F32)).astype(BF16)
    row = lax.broadcasted_iota(jnp.int32, (16, CH), 0)
    wide = jnp.where(row == 0, top.astype(F32), jnp.where(row == 1, mid.astype(F32), low.astype(F32)))
    send[5 * CELLS :, :] = wide.astype(BF16)


def term_kernel(me, offs, basis, left, own, right, fwd, got, term, term16, packed, ext, rows):
    fill_ext(ext, left, own, right)
    squares = jnp.zeros((CELLS, 1), F32)
    inner = jnp.zeros((CELLS, 1), F32)
    for j in range(NCHAN):
        norm = got[0, CELLS * j : CELLS * (j + 1), :].astype(F32)
        for h in range(1, NCHAN):
            norm += got[h, CELLS * j : CELLS * (j + 1), :].astype(F32)
        f = got[j, 4 * CELLS : 5 * CELLS, :].astype(F32)
        g3 = got[j, 5 * CELLS :, :].astype(F32)
        g = g3[0:1] + g3[1:2] + g3[2:3]
        squares += jnp.sum(f * f, axis=1, keepdims=True)
        inner += jnp.sum(f * (g * norm), axis=1, keepdims=True)
    mine = pl.ds(pl.multiple_of(me[0] * CELLS, CELLS), CELLS)
    norm = got[0, mine, :].astype(F32)
    for h in range(1, NCHAN):
        norm += got[h, mine, :].astype(F32)
    g3 = got[me[0], 5 * CELLS :, :].astype(F32)
    g = g3[0:1] + g3[1:2] + g3[2:3]
    inv_rms = lax.rsqrt(squares / D + EPSILON)
    f = fwd[...]
    ft = inv_rms * (g * norm) - f * (inv_rms * inv_rms * inv_rms * (inner / D))
    term[...] = ft
    term16[...] = ft.astype(BF16)
    gain_row = jnp.sum(norm * f * inv_rms, axis=0, keepdims=True)
    rows[...] = jnp.zeros((2, 24, 128), F32)
    rows[0, 20:21, :] = gain_row[:, :128]
    rows[1, 20:21, : CH - 128] = gain_row[:, 128:]
    pad = jnp.zeros((LON, 256 - CH), F32)
    for k in range(TAPS):
        lo = jnp.zeros((LON, 128), F32)
        hi = jnp.zeros((LON, 128), F32)
        for r in range(ROWS):
            src = r + k // PER_ROW - REACH
            if 0 <= src < ROWS:
                at = pl.ds(EXT * src + LON + offs[r, k], LON)
                lo += basis[r, k] * (ft[LON * r : LON * (r + 1), :128] * ext[0, at, :])
                wide = jnp.concatenate([ft[LON * r : LON * (r + 1), 128:], pad], axis=1)
                hi += basis[r, k] * (wide * ext[1, at, :])
        rows[0, k : k + 1, :] = jnp.sum(lo, axis=0, keepdims=True)
        rows[1, k : k + 1, :] = jnp.sum(hi, axis=0, keepdims=True)
    first = rows[0, 0:21, :]
    second = rows[1, 0:HALF, :] + pltpu.roll(rows[1, HALF : 2 * HALF, :], 64, 1)
    value = jnp.concatenate([first, second], axis=0).astype(BF16)
    for i in range(8):
        packed[i] = value


def sum_kernel(got, out):
    total = got[0].astype(F32)
    for i in range(1, 8):
        total += got[i].astype(F32)
    total = total.astype(BF16)
    for i in range(16):
        out[i] = total


def final_kernel(offs, basis, left, term, right, taps, cot, got, grad, gain_grad, tap_grad, ext, total):
    fill_ext(ext, left, term, right)
    for r2 in range(ROWS):
        lo = jnp.zeros((LON, 128), F32)
        hi = jnp.zeros((LON, 128), F32)
        for k in range(TAPS):
            r = r2 - (k // PER_ROW - REACH)
            if 0 <= r < ROWS:
                at = pl.ds(EXT * r + LON - offs[r, k], LON)
                lo += basis[r, k] * (taps[k : k + 1, :128] * ext[0, at, :])
                hi += basis[r, k] * (taps[k : k + 1, 128:] * ext[1, at, :])
        total[LON * r2 : LON * (r2 + 1), :128] = lo
        total[LON * r2 : LON * (r2 + 1), 128:] = hi[:, : CH - 128]
    grad[...] = (cot[...].astype(F32) + total[...]).astype(BF16)
    value = got[0].astype(F32)
    for i in range(1, 16):
        value += got[i].astype(F32)
    value = value * SCALE
    tap_grad[:, :128] = value[0:TAPS]
    gain_grad[:, :128] = value[TAPS : TAPS + 1]
    back = pltpu.roll(value[21:32], 64, 1)
    tap_grad[0:HALF, 128:] = value[21:32, : CH - 128]
    tap_grad[HALF:TAPS, 128:] = back[0 : TAPS - HALF, : CH - 128]
    gain_grad[:, 128:] = back[TAPS - HALF : TAPS - HALF + 1, : CH - 128]


def shape(dims, dtype=F32):
    return jax.ShapeDtypeStruct(dims, dtype)


def both_ways(value):
    n = 128
    left = lax.ppermute(value, GRID, [(i, (i + 1) % n) for i in range(n)])
    right = lax.ppermute(value, GRID, [(i, (i - 1) % n) for i in range(n)])
    return left, right


def per_device(field, cotangent, pre_hidden, w_up, w_down, gain, tap_weights, basis, lon_offsets):
    field = field.reshape(CELLS, CH)
    cot = cotangent.reshape(CELLS, CH)
    pre = pre_hidden.reshape(CELLS, HID)
    taps = jnp.pad(tap_weights, ((0, 0), (0, 256 - CH)))
    me = lax.axis_index("chan").astype(jnp.int32).reshape(1)
    left, right = both_ways(field)
    cot_all = lax.all_gather(cot, "chan")
    part = pl.pallas_call(
        mlp_kernel,
        out_shape=shape((4 * CELLS, CH), BF16),
        in_specs=[VMEM] * 4,
        out_specs=VMEM,
        scratch_shapes=[pltpu.VMEM((CELLS, D), BF16)],
        compiler_params=params(),
        name="mlp",
    )(cot_all, pre, w_down, w_up)
    fwd, send = pl.pallas_call(
        forward_kernel,
        out_shape=(shape((CELLS, CH)), shape((SEND, CH), BF16)),
        in_specs=[SMEM, SMEM] + [VMEM] * 6,
        out_specs=(VMEM, VMEM),
        scratch_shapes=[pltpu.VMEM((2, ROWS * EXT, 128), F32)],
        compiler_params=params(),
        name="forward",
    )(lon_offsets, basis, left, field, right, taps, gain.reshape(1, CH), part)
    got = lax.all_gather(send, "chan")
    term, term16, packed = pl.pallas_call(
        term_kernel,
        out_shape=(shape((CELLS, CH)), shape((CELLS, CH), BF16), shape((8, PACK, 128), BF16)),
        in_specs=[SMEM] * 3 + [VMEM] * 5,
        out_specs=(VMEM,) * 3,
        scratch_shapes=[pltpu.VMEM((2, ROWS * EXT, 128), F32), pltpu.VMEM((2, 24, 128), F32)],
        compiler_params=params(),
        name="term",
    )(me, lon_offsets, basis, left, field, right, fwd, got)
    term_left, term_right = both_ways(term16)
    over_z = lax.all_to_all(packed, "z", 0, 0)
    again = pl.pallas_call(
        sum_kernel,
        out_shape=shape((16, PACK, 128), BF16),
        in_specs=[VMEM],
        out_specs=VMEM,
        compiler_params=params(),
        name="zsum",
    )(over_z)
    over_yx = lax.all_to_all(again, ("y", "xh"), 0, 0)
    grad, gain_grad, tap_grad = pl.pallas_call(
        final_kernel,
        out_shape=(shape((CELLS, CH), BF16), shape((1, CH)), shape((TAPS, CH))),
        in_specs=[SMEM, SMEM] + [VMEM] * 6,
        out_specs=(VMEM,) * 3,
        scratch_shapes=[pltpu.VMEM((2, ROWS * EXT, 128), F32), pltpu.VMEM((CELLS, CH), F32)],
        compiler_params=params(),
        name="final",
    )(lon_offsets, basis, term_left, term, term_right, taps, cot, over_yx)
    return (grad.reshape(ROWS, LON, CH), gain_grad.reshape(CH), tap_grad)


def solution(mesh):
    fine = Mesh(mesh.devices.reshape(8, 8, 2, NCHAN), (*GRID, "chan"))
    cells = P(None, GRID, "chan")
    placed = (
        cells,
        cells,
        cells,
        P(None, "chan"),
        P("chan", None),
        P("chan"),
        P(None, "chan"),
        P(),
        P(),
    )
    return jax.shard_map(
        per_device,
        mesh=fine,
        in_specs=placed,
        out_specs=(cells, P("chan"), P(None, "chan")),
        check_vma=False,
    )
```

time: 818 us -> 80.8 us (0.10)
  the two profiles are of different devices: /device:TPU:2 before, /device:TPU:30 now
where the time goes in v1:
time: 80.8 us; the launch traced here: 80.3 us
  blocking collectives  34.9 us (43%)
  starting transfers between devices  25 us (31%)
  waiting for transfers between devices  7.01 us (9%)
  Pallas kernels  6.43 us (8%)
  local copies, waits for them, and re-layouts  6.14 us (8%)
    all_to_all x1, blocking collectives, per_device(): over_z = lax.all_to_all(packed, 'z', 0, 0)  18.5 us
    all_gather x1, blocking collectives, per_device(): got = lax.all_gather(send, 'chan')  10.9 us
    all_to_all x1, starting transfers between devices, per_device(): over_yx = lax.all_to_all(again, ('y', 'xh'), 0, 0)  10.2 us
    ppermute x2, starting transfers between devices, both_ways(): left = lax.ppermute(value, GRID, [(i, (i + 1) % n) for i in range(n)])  10.1 us
    ppermute x2, waiting for transfers between devices, both_ways(): right = lax.ppermute(value, GRID, [(i, (i - 1) % n) for i in range(n)])  6.7 us
    all_gather x1, blocking collectives, per_device(): cot_all = lax.all_gather(cot, 'chan')  5.61 us
    ppermute x2, starting transfers between devices, both_ways(): right = lax.ppermute(value, GRID, [(i, (i - 1) % n) for i in range(n)])  4.69 us
    unnamed x17, local copies, waits for them, and re-layouts  3.64 us
  transfers between devices with their start and end apart: 5, of which 2 were waited for; matrix products, arithmetic and copies ran while one was open for 2% of the time, Pallas kernels for 1%

profile of v1, /device:TPU:30, one launch (start us, length us, event | category | flops | bytes accessed | tf_op | source)
XLA Modules:
  0.0 80.3 jit_solution(16870267854344675876)
XLA Ops:
  0.6 5.5 %collective-permute-start = (bf16[128,192]{1,0:T(8,128)(2,1)}, bf16[128,192]{1,0:T(8,128)(2,1)S(1)}, u32[]{:S(2)}, u32[]{:S(2)}) collective-permute-start(bf16[128,192]{1,0:T(8,128)(2,1)} %bitcast.10), channel_id=1, source_target_pairs={{0,4},{4,8},{8,12},{12,16},{16,20},{20,24},{24,28},{28,32},{32,36}... | collective-permute-start | bytes 147464 | tf_op jit(solution)/shard_map/ppermute | solution.py:193
  6.2 1.9 %collective-permute-start.1 = (bf16[128,192]{1,0:T(8,128)(2,1)}, bf16[128,192]{1,0:T(8,128)(2,1)S(1)}, u32[]{:S(2)}, u32[]{:S(2)}) collective-permute-start(bf16[128,192]{1,0:T(8,128)(2,1)} %bitcast.11), channel_id=1, source_target_pairs={{0,508},{4,0},{8,4},{12,8},{16,12},{20,16},{24,20},{28,24},{32,28}... | collective-permute-start | bytes 147464 | tf_op jit(solution)/shard_map/ppermute | solution.py:194
  8.1 0.9 %copy.16 = bf16[1,128,192]{1,2,0:T(8,128)(2,1)S(1)} copy(bf16[1,128,192]{2,1,0:T(8,128)(2,1)} %bitcast.14) | data formatting | bytes 98304 | tf_op jit(solution)/shard_map/all_gather;reshape | solution.py:205
  9.1 5.6 %all_gather.9 = bf16[4,128,192]{1,2,0:T(8,128)(2,1)S(1)} all-gather(bf16[1,128,192]{1,2,0:T(8,128)(2,1)S(1)} %copy.16), channel_id=1, replica_groups=mesh['z'=8,'y'=8,'xh'=2,'chan'=4] {'chan'}, dimensions={0}, use_global_device_ids=true | all-gather | bytes 245760 | tf_op jit(solution)/shard_map/all_gather | solution.py:205
  14.7 0.1 copy.17.cot
  14.8 0.7 pad.4.taps
  15.6 0.0 copy-start
  15.6 1.3 %copy-done = bf16[768,768]{1,0:T(8,128)(2,1)S(1)} copy-done((bf16[768,768]{1,0:T(8,128)(2,1)S(1)}, bf16[768,768]{1,0:T(8,128)(2,1)}, u32[]{:S(2)}) %copy-start) | copy-done | bytes 1179672
  16.8 0.0 copy-start.1
  16.8 1.3 %copy-done.1 = bf16[768,768]{1,0:T(8,128)(2,1)S(1)} copy-done((bf16[768,768]{1,0:T(8,128)(2,1)S(1)}, bf16[768,768]{1,0:T(8,128)(2,1)}, u32[]{:S(2)}) %copy-start.1) | copy-done | bytes 1179672
  18.1 0.0 copy-start.4
  18.1 0.9 %copy-done.4 = bf16[16,8,768]{2,1,0:T(8,128)(2,1)S(1)} copy-done((bf16[16,8,768]{2,1,0:T(8,128)(2,1)S(1)}, bf16[16,8,768]{2,1,0:T(8,128)(2,1)}, u32[]{:S(2)}) %copy-start.4) | copy-done | bytes 196632
  19.0 0.0 copy-start.2
  19.0 0.0 copy-start.5
  19.0 0.0 copy-start.6
  19.0 0.0 copy-start.7
  19.0 1.1 %mlp.1.part = bf16[512,192]{1,0:T(8,128)(2,1)S(1)} custom-call(bf16[4,128,192]{2,1,0:T(8,128)(2,1)S(1)} %copy.17.cot, bf16[128,768]{1,0:T(8,128)(2,1)S(1)} %bitcast.16, bf16[768,768]{1,0:T(8,128)(2,1)S(1)} %copy-done, bf16[768,768]{1,0:T(8,128)(2,1)S(1)} %copy-done.1), custom_call_target="tpu_custom_call" | custom-call | tf_op jit(solution)/shard_map/mlp/pallas_call | solution.py:206
  20.1 0.0 collective-permute-done.left
  20.1 0.0 collective-permute-done.1.right
  20.1 0.0 copy-done.2
  20.2 0.0 copy-done.5
  20.2 0.0 copy-done.6
  20.2 0.0 copy-done.7
  20.2 1.2 %forward.1 = (f32[128,192]{1,0:T(8,128)S(1)}, bf16[656,192]{1,0:T(8,128)(2,1)S(1)}) custom-call(s32[16,20]{1,0:T(8,128)S(1)} %copy-done.5, f32[16,20]{1,0:T(8,128)S(1)} %copy-done.6, bf16[128,192]{1,0:T(8,128)(2,1)S(1)} %collective-permute-done.left, bf16[128,192]{1,0:T(8,128)(2,1)S(1)} %bitcast.12, bf16[128,192]{1,0:T(8,128)(2,1)S(1)} %collective-permute-done.1.right, ...), custom_call_target="tpu_custom_call" | custom-call | tf_op jit(solution)/shard_map/forward/pallas_call | solution.py:215
  21.4 0.2 copy.18
  21.6 10.9 %all-gather.1 = bf16[4,656,192]{1,2,0:T(8,128)(2,1)S(1)} all-gather(bf16[1,656,192]{1,2,0:T(8,128)(2,1)S(1)} %copy.18), channel_id=2, replica_groups=mesh['z'=8,'y'=8,'xh'=2,'chan'=4] {'chan'}, dimensions={0}, use_global_device_ids=true | all-gather | bytes 1259520 | tf_op jit(solution)/shard_map/all_gather | solution.py:224
  32.4 0.7 copy.19.got
  33.1 0.0 copy-start.3
  33.1 1.6 %term.1 = (f32[128,192]{1,0:T(8,128)S(1)}, bf16[128,192]{1,0:T(8,128)(2,1)S(1)}, bf16[8,32,128]{2,1,0:T(8,128)(2,1)S(1)}) custom-call(s32[1]{0:T(128)} %bitcast.me, s32[16,20]{1,0:T(8,128)S(1)} %copy-done.5, f32[16,20]{1,0:T(8,128)S(1)} %copy-done.6, bf16[128,192]{1,0:T(8,128)(2,1)S(1)} %collective-permute-done.left, bf16[128,192]{1,0:T(8,128)(2,1)S(1)} %bitcast.13, ...), custom_call_target="tpu_custom_call" | custom-call | tf_op jit(solution)/shard_map/term/pallas_call | solution.py:225
  34.7 18.5 %all_to_all.10.got = bf16[8,32,128]{2,1,0:T(8,128)(2,1)S(1)} all-to-all(bf16[8,32,128]{2,1,0:T(8,128)(2,1)S(1)} %get-tuple-element.15), channel_id=1, replica_groups=mesh['z'=8,'y'=8,'xh'=2,'chan'=4] {'z'}, dimensions={0} | all-to-all | bytes 131072 | tf_op jit(solution)/shard_map/all_to_all | solution.py:235
  53.2 0.7 zsum.1
  53.9 10.2 %all-to-all-start.1 = ((bf16[16,32,128]{2,1,0:T(8,128)(2,1)}), bf16[16,32,128]{2,1,0:T(8,128)(2,1)S(1)}, u32[]{:S(2)}, u32[]{:S(2)}) async-start(bf16[16,32,128]{2,1,0:T(8,128)(2,1)} %zsum.1), calls=%async_computation.1 | async-start | bytes 262144 | tf_op jit(solution)/shard_map/all_to_all | solution.py:244
  64.1 4.6 %collective-permute-start.2 = (bf16[128,192]{1,0:T(8,128)(2,1)S(1)}, bf16[128,192]{1,0:T(8,128)(2,1)S(1)}, u32[]{:S(2)}, u32[]{:S(2)}) collective-permute-start(bf16[128,192]{1,0:T(8,128)(2,1)S(1)} %get-tuple-element.13), channel_id=1, source_target_pairs={{0,4},{4,8},{8,12},{12,16},{16,20},{20,24},{24,28},{28,32},{32,36}... | collective-permute-start | bytes 147464 | tf_op jit(solution)/shard_map/ppermute | solution.py:193
  68.6 2.8 %collective-permute-start.3 = (bf16[128,192]{1,0:T(8,128)(2,1)S(1)}, bf16[128,192]{1,0:T(8,128)(2,1)S(1)}, u32[]{:S(2)}, u32[]{:S(2)}) collective-permute-start(bf16[128,192]{1,0:T(8,128)(2,1)S(1)} %get-tuple-element.13), channel_id=1, source_target_pairs={{0,508},{4,0},{8,4},{12,8},{16,12},{20,16},{24,20},{28,24},{32,28}... | collective-permute-start | bytes 147464 | tf_op jit(solution)/shard_map/ppermute | solution.py:194
  71.4 0.3 collective-permute-done.2.left
  71.7 6.7 %collective-permute-done.3.right = bf16[128,192]{1,0:T(8,128)(2,1)S(1)} collective-permute-done((bf16[128,192]{1,0:T(8,128)(2,1)S(1)}, bf16[128,192]{1,0:T(8,128)(2,1)S(1)}, u32[]{:S(2)}, u32[]{:S(2)}) %collective-permute-start.3) | collective-permute-done | bytes 49184 | tf_op jit(solution)/shard_map/ppermute | solution.py:194
  78.4 0.0 all-to-all-done.1.got
  78.4 0.0 copy-done.3
  78.4 1.8 %final.1 = (bf16[128,192]{1,0:T(8,128)(2,1)}, f32[1,192]{1,0:T(1,128)}, f32[20,192]{1,0:T(8,128)}) custom-call(s32[16,20]{1,0:T(8,128)S(1)} %copy-done.5, f32[16,20]{1,0:T(8,128)S(1)} %copy-done.6, bf16[128,192]{1,0:T(8,128)(2,1)S(1)} %collective-permute-done.2.left, f32[128,192]{1,0:T(8,128)S(1)} %get-tuple-element.14.term, ...), custom_call_target="tpu_custom_call" | custom-call | tf_op jit(solution)/shard_map/final/pallas_call | solution.py:245
Async XLA Ops:
  0.6 19.5 %collective-permute-start = (bf16[128,192]{1,0:T(8,128)(2,1)}, bf16[128,192]{1,0:T(8,128)(2,1)S(1)}, u32[]{:S(2)}, u32[]{:S(2)}) collective-permute-start(bf16[128,192]{1,0:T(8,128)(2,1)} %bitcast.10), channel_id=1, source_target_pairs={{0,4},{4,8},{8,12},{12,16},{16,20},{20,24},{24,28},{28,32},{32,36}... | collective-permute-start | bytes 147464 | tf_op jit(solution)/shard_map/ppermute | solution.py:193
  6.2 14.0 %collective-permute-start.1 = (bf16[128,192]{1,0:T(8,128)(2,1)}, bf16[128,192]{1,0:T(8,128)(2,1)S(1)}, u32[]{:S(2)}, u32[]{:S(2)}) collective-permute-start(bf16[128,192]{1,0:T(8,128)(2,1)} %bitcast.11), channel_id=1, source_target_pairs={{0,508},{4,0},{8,4},{12,8},{16,12},{20,16},{24,20},{28,24},{32,28}... | collective-permute-start | bytes 147464 | tf_op jit(solution)/shard_map/ppermute | solution.py:194
  15.6 1.3 %copy-start = (bf16[768,768]{1,0:T(8,128)(2,1)S(1)}, bf16[768,768]{1,0:T(8,128)(2,1)}, u32[]{:S(2)}) copy-start(bf16[768,768]{1,0:T(8,128)(2,1)} %w_down.1) | copy-start | bytes 3538948
  16.8 1.3 %copy-start.1 = (bf16[768,768]{1,0:T(8,128)(2,1)S(1)}, bf16[768,768]{1,0:T(8,128)(2,1)}, u32[]{:S(2)}) copy-start(bf16[768,768]{1,0:T(8,128)(2,1)} %w_up.1) | copy-start | bytes 3538948
  18.1 0.9 %copy-start.4 = (bf16[16,8,768]{2,1,0:T(8,128)(2,1)S(1)}, bf16[16,8,768]{2,1,0:T(8,128)(2,1)}, u32[]{:S(2)}) copy-start(bf16[16,8,768]{2,1,0:T(8,128)(2,1)} %param.11) | copy-start | bytes 589828
  19.0 1.1 %copy-start.2 = (bf16[16,8,192]{2,1,0:T(8,128)(2,1)S(1)}, bf16[16,8,192]{2,1,0:T(8,128)(2,1)}, u32[]{:S(2)}) copy-start(bf16[16,8,192]{2,1,0:T(8,128)(2,1)} %param.9) | copy-start | bytes 147460
  19.0 1.1 %copy-start.5 = (s32[16,20]{1,0:T(8,128)S(1)}, s32[16,20]{1,0:T(8,128)}, u32[]{:S(2)}) copy-start(s32[16,20]{1,0:T(8,128)} %offs.5) | copy-start | bytes 3844
  19.0 1.1 %copy-start.6 = (f32[16,20]{1,0:T(8,128)S(1)}, f32[16,20]{1,0:T(8,128)}, u32[]{:S(2)}) copy-start(f32[16,20]{1,0:T(8,128)} %basis.5) | copy-start | bytes 3844
  19.0 1.1 %copy-start.7 = (f32[192]{0:T(256)S(1)}, f32[192]{0:T(256)}, u32[]{:S(2)}) copy-start(f32[192]{0:T(256)} %param.14) | copy-start | bytes 2308
  33.1 45.3 %copy-start.3 = (bf16[16,8,192]{2,1,0:T(8,128)(2,1)S(1)}, bf16[16,8,192]{2,1,0:T(8,128)(2,1)}, u32[]{:S(2)}) copy-start(bf16[16,8,192]{2,1,0:T(8,128)(2,1)} %param.10) | copy-start | bytes 147460
  53.9 24.5 %all-to-all-start.1 = ((bf16[16,32,128]{2,1,0:T(8,128)(2,1)}), bf16[16,32,128]{2,1,0:T(8,128)(2,1)S(1)}, u32[]{:S(2)}, u32[]{:S(2)}) async-start(bf16[16,32,128]{2,1,0:T(8,128)(2,1)} %zsum.1), calls=%async_computation.1 | async-start | bytes 262144 | tf_op jit(solution)/shard_map/all_to_all | solution.py:244
  64.1 7.7 %collective-permute-start.2 = (bf16[128,192]{1,0:T(8,128)(2,1)S(1)}, bf16[128,192]{1,0:T(8,128)(2,1)S(1)}, u32[]{:S(2)}, u32[]{:S(2)}) collective-permute-start(bf16[128,192]{1,0:T(8,128)(2,1)S(1)} %get-tuple-element.13), channel_id=1, source_target_pairs={{0,4},{4,8},{8,12},{12,16},{16,20},{20,24},{24,28},{28,32},{32,36}... | collective-permute-start | bytes 147464 | tf_op jit(solution)/shard_map/ppermute | solution.py:193
  68.6 9.8 %collective-permute-start.3 = (bf16[128,192]{1,0:T(8,128)(2,1)S(1)}, bf16[128,192]{1,0:T(8,128)(2,1)S(1)}, u32[]{:S(2)}, u32[]{:S(2)}) collective-permute-start(bf16[128,192]{1,0:T(8,128)(2,1)S(1)} %get-tuple-element.13), channel_id=1, source_target_pairs={{0,508},{4,0},{8,4},{12,8},{16,12},{20,16},{24,20},{28,24},{32,28}... | collective-permute-start | bytes 147464 | tf_op jit(solution)/shard_map/ppermute | solution.py:194

commit v2 on v1

v2 whole, which is shorter than its diff:
```python
import math

import jax
import jax.numpy as jnp
from jax import lax
from jax.experimental import pallas as pl
from jax.experimental.pallas import tpu as pltpu
from jax.sharding import Mesh
from jax.sharding import PartitionSpec as P

ROWS = 16
LON = 8
CELLS = ROWS * LON
D = 768
CH = 192
HID = 768
TAPS = 20
REACH = 2
PER_ROW = 4
NCHAN = 4
EXT = 3 * LON
GRID = ("z", "y", "xh")

EPSILON = 1e-05
INV_SQRT_TWO = 0.7071067811865476
INV_SQRT_TWO_PI = 0.3989422804014327
SCALE = 1.0 / math.sqrt(16384.0)

F32 = jnp.float32
BF16 = jnp.bfloat16
NT = (((1,), (1,)), ((), ()))

FWD_AT = D
SQ_AT = D + CH
SEND = SQ_AT + 16
PACK = 32
HALF = 11

VMEM = pl.BlockSpec(memory_space=pltpu.VMEM)
SMEM = pl.BlockSpec(memory_space=pltpu.SMEM)
HBM = pl.BlockSpec(memory_space=pltpu.HBM)


def call(kernel, outs, ins, out_specs, scratch, name, flops=0, moved=0, limit=24):
    return pl.pallas_call(
        kernel,
        out_shape=outs,
        in_specs=ins,
        out_specs=out_specs,
        scratch_shapes=scratch,
        compiler_params=pltpu.CompilerParams(vmem_limit_bytes=limit * 1024 * 1024),
        cost_estimate=pl.CostEstimate(flops=flops, bytes_accessed=moved, transcendentals=0),
        name=name,
    )


def taps_from(row):
    out = []
    for k in range(TAPS):
        src = row + k // PER_ROW - REACH
        if 0 <= src < ROWS:
            out.append((k, src))
    return out


def fill_own(ext, ref):
    v = ref[...].astype(F32)
    for r in range(ROWS):
        to = pl.ds(EXT * r + LON, LON)
        ext[0, to, :] = v[LON * r : LON * r + LON, :128]
        ext[1, to, : CH - 128] = v[LON * r : LON * r + LON, 128:]


def fill_side(ext, ref, start):
    v = ref[...].astype(F32)
    for r in range(ROWS):
        to = pl.ds(pl.multiple_of(EXT * r + start, LON), LON)
        ext[0, to, :] = v[LON * r : LON * r + LON, :128]
        ext[1, to, : CH - 128] = v[LON * r : LON * r + LON, 128:]


def fill_ext(ext, place, own, near, far):
    ext[1] = jnp.zeros((ROWS * EXT, 128), F32)
    start = 2 * LON * (1 - (place[0] >> 2))
    fill_own(ext, own)
    fill_side(ext, near, start)
    fill_side(ext, far, 2 * LON - start)


def prep_kernel(cot, out):
    turned = cot[...].astype(F32).T.astype(BF16)
    for i in range(NCHAN):
        out[i] = turned


def ready_kernel(pre, gain, taps, slope, gain_t, wide):
    v = pre[...].astype(F32)
    s = (
        0.5 * (1.0 + lax.erf(v * INV_SQRT_TWO))
        + v * jnp.exp(-0.5 * v * v) * INV_SQRT_TWO_PI
    )
    slope[...] = s.T
    gain_t[...] = jnp.broadcast_to(gain[...], (CELLS, CH)).T
    wide[...] = jnp.zeros((TAPS, 256), F32)
    wide[:, :CH] = taps[...]


def mlp_kernel(cot, slope, down, up, out):
    hidden = jnp.dot(down[...], cot[...], preferred_element_type=F32)
    grad = (hidden * slope[...]).astype(BF16)
    out[...] = jnp.dot(up[...], grad, preferred_element_type=F32).astype(BF16)


def forward_kernel(place, offs, basis, own, near, far, taps, gain_t, part, fwd_t, send, ext, fwd):
    fill_ext(ext, place, own, near, far)
    for r in range(ROWS):
        lo = jnp.zeros((LON, 128), F32)
        hi = jnp.zeros((LON, 128), F32)
        for k, src in taps_from(r):
            at = pl.ds(EXT * src + LON + offs[r, k], LON)
            lo += basis[r, k] * (taps[k : k + 1, :128] * ext[0, at, :])
            hi += basis[r, k] * (taps[k : k + 1, 128:] * ext[1, at, :])
        fwd[LON * r : LON * (r + 1), :128] = lo
        fwd[LON * r : LON * (r + 1), 128:] = hi[:, : CH - 128]
    f = fwd[...].T
    fwd_t[...] = f
    send[:FWD_AT, :] = part[...]
    send[FWD_AT:SQ_AT, :] = (gain_t[...] * f).astype(BF16)
    sq = jnp.sum(f * f, axis=0, keepdims=True)
    top = sq.astype(BF16).astype(F32)
    mid = (sq - top).astype(BF16).astype(F32)
    row = lax.broadcasted_iota(jnp.int32, (16, CELLS), 0)
    three = jnp.where(row == 0, top, jnp.where(row == 1, mid, sq - top - mid))
    send[SQ_AT:, :] = three.astype(BF16)


def term_kernel(place, offs, basis, ext, fwd_t, gain_t, got, term, term16, packed, rows):
    inner = jnp.zeros((1, CELLS), F32)
    squares = jnp.zeros((1, CELLS), F32)
    for j in range(NCHAN):
        norm = got[0, CH * j : CH * (j + 1), :].astype(F32)
        for h in range(1, NCHAN):
            norm += got[h, CH * j : CH * (j + 1), :].astype(F32)
        f = got[j, FWD_AT:SQ_AT, :].astype(F32)
        inner += jnp.sum(f * norm, axis=0, keepdims=True)
        three = got[j, SQ_AT:, :].astype(F32)
        squares += three[0:1] + three[1:2] + three[2:3]
    mine = pl.ds(pl.multiple_of((place[0] & 3) * CH, CH), CH)
    norm = got[0, mine, :].astype(F32)
    for h in range(1, NCHAN):
        norm += got[h, mine, :].astype(F32)
    inv_rms = lax.rsqrt(squares / D + EPSILON)
    f = fwd_t[...]
    scaled = inv_rms * norm
    ft = (gain_t[...] * scaled - f * (inv_rms * inv_rms * inv_rms * (inner / D))).T
    term[...] = ft
    term16[...] = ft.astype(BF16)
    gain_row = jnp.sum((scaled * f).T, axis=0, keepdims=True)
    rows[...] = jnp.zeros((2, 24, 128), F32)
    rows[0, 20:21, :] = gain_row[:, :128]
    rows[1, 20:21, : CH - 128] = gain_row[:, 128:]
    pad = jnp.zeros((LON, 256 - CH), F32)
    for k in range(TAPS):
        lo = jnp.zeros((LON, 128), F32)
        hi = jnp.zeros((LON, 128), F32)
        for r in range(ROWS):
            src = r + k // PER_ROW - REACH
            if 0 <= src < ROWS:
                at = pl.ds(EXT * src + LON + offs[r, k], LON)
                lo += basis[r, k] * (ft[LON * r : LON * (r + 1), :128] * ext[0, at, :])
                wide = jnp.concatenate([ft[LON * r : LON * (r + 1), 128:], pad], axis=1)
                hi += basis[r, k] * (wide * ext[1, at, :])
        rows[0, k : k + 1, :] = jnp.sum(lo, axis=0, keepdims=True)
        rows[1, k : k + 1, :] = jnp.sum(hi, axis=0, keepdims=True)
    first = rows[0, 0:21, :]
    second = rows[1, 0:HALF, :] + pltpu.roll(rows[1, HALF : 2 * HALF, :], 64, 1)
    value = jnp.concatenate([first, second], axis=0).astype(BF16)
    for i in range(16):
        packed[i] = value


def resum_kernel(got, out):
    total = got[0].astype(F32)
    for i in range(1, 16):
        total += got[i].astype(F32)
    total = total.astype(BF16)
    for i in range(8):
        out[i] = total


def adjoint_kernel(place, offs, basis, own, near, far, taps, cot, grad, ext, total):
    fill_ext(ext, place, own, near, far)
    for r2 in range(ROWS):
        lo = jnp.zeros((LON, 128), F32)
        hi = jnp.zeros((LON, 128), F32)
        for k in range(TAPS):
            r = r2 - (k // PER_ROW - REACH)
            if 0 <= r < ROWS:
                at = pl.ds(EXT * r + LON - offs[r, k], LON)
                lo += basis[r, k] * (taps[k : k + 1, :128] * ext[0, at, :])
                hi += basis[r, k] * (taps[k : k + 1, 128:] * ext[1, at, :])
        total[LON * r2 : LON * (r2 + 1), :128] = lo
        total[LON * r2 : LON * (r2 + 1), 128:] = hi[:, : CH - 128]
    grad[...] = (cot[...].astype(F32) + total[...]).astype(BF16)


def last_kernel(got, gain_grad, tap_grad):
    value = got[0].astype(F32)
    for i in range(1, 8):
        value += got[i].astype(F32)
    value = value * SCALE
    tap_grad[:, :128] = value[0:TAPS]
    gain_grad[:, :128] = value[TAPS : TAPS + 1]
    back = pltpu.roll(value[21:32], 64, 1)
    tap_grad[0:HALF, 128:] = value[21:32, : CH - 128]
    tap_grad[HALF:TAPS, 128:] = back[0 : TAPS - HALF, : CH - 128]
    gain_grad[:, 128:] = back[TAPS - HALF : TAPS - HALF + 1, : CH - 128]


def shape(dims, dtype=F32):
    return jax.ShapeDtypeStruct(dims, dtype)


def swap_near(value):
    return lax.ppermute(value, "xh", [(0, 1), (1, 0)])


def swap_far(value):
    n = 128
    return lax.ppermute(value, GRID, [(i, (i + 1 if i % 2 else i - 1) % n) for i in range(n)])


def per_device(field, cotangent, pre_hidden, w_up, w_down, gain, tap_weights, basis, lon_offsets):
    field = field.reshape(CELLS, CH)
    cot = cotangent.reshape(CELLS, CH)
    pre = pre_hidden.reshape(CELLS, HID)
    place = lax.axis_index(("xh", "chan")).astype(jnp.int32).reshape(1)
    ext_shape = (2, ROWS * EXT, 128)

    cots = call(prep_kernel, shape((NCHAN, CH, CELLS), BF16), [VMEM], VMEM, [], "prep", flops=8_000_000_000)(cot)
    cot_all = lax.all_to_all(cots, "chan", 0, 0).reshape(D, CELLS)
    near, far = swap_near(field), swap_far(field)
    slope, gain_t, taps = call(
        ready_kernel,
        (shape((HID, CELLS)), shape((CH, CELLS)), shape((TAPS, 256))),
        [VMEM] * 3,
        (VMEM,) * 3,
        [],
        "ready",
        moved=3_000_000,
    )(pre, gain.reshape(1, CH), tap_weights)
    part = call(mlp_kernel, shape((D, CELLS), BF16), [VMEM] * 4, VMEM, [], "mlp", flops=300_000_000)(
        cot_all, slope, w_down, w_up
    )
    fwd_t, send, ext = call(
        forward_kernel,
        (shape((CH, CELLS)), shape((SEND, CELLS), BF16), shape(ext_shape)),
        [SMEM] * 3 + [VMEM] * 6,
        (VMEM,) * 3,
        [pltpu.VMEM((CELLS, CH), F32)],
        "forward",
    )(place, lon_offsets, basis, field, near, far, taps, gain_t, part)
    got = lax.all_gather(send, "chan")
    term, term16, packed = call(
        term_kernel,
        (shape((CELLS, CH)), shape((CELLS, CH), BF16), shape((16, PACK, 128), BF16)),
        [SMEM] * 3 + [VMEM] * 4,
        (VMEM,) * 3,
        [pltpu.VMEM((2, 24, 128), F32)],
        "term",
    )(place, lon_offsets, basis, ext, fwd_t, gain_t, got)
    over_yx = lax.all_to_all(packed, ("y", "xh"), 0, 0)
    term_far = swap_far(term16)
    over_yx, term_far, term_again = lax.optimization_barrier((over_yx, term_far, term16))
    again = call(resum_kernel, shape((8, PACK, 128), BF16), [VMEM], VMEM, [], "resum")(over_yx)
    over_z = lax.all_to_all(again, "z", 0, 0)
    term_near = swap_near(term_again)
    grad = call(
        adjoint_kernel,
        shape((CELLS, CH), BF16),
        [SMEM] * 3 + [VMEM] * 5,
        VMEM,
        [pltpu.VMEM(ext_shape, F32), pltpu.VMEM((CELLS, CH), F32)],
        "adjoint",
        moved=6_000_000,
    )(place, lon_offsets, basis, term, term_near, term_far, taps, cot)
    gain_grad, tap_grad = call(
        last_kernel, (shape((1, CH)), shape((TAPS, CH))), [VMEM], (VMEM,) * 2, [], "last"
    )(over_z)
    return (grad.reshape(ROWS, LON, CH), gain_grad.reshape(CH), tap_grad)


def solution(mesh):
    fine = Mesh(mesh.devices.reshape(8, 8, 2, NCHAN), (*GRID, "chan"))
    cells = P(None, GRID, "chan")
    placed = (
        cells,
        cells,
        cells,
        P(None, "chan"),
        P("chan", None),
        P("chan"),
        P(None, "chan"),
        P(),
        P(),
    )
    return jax.shard_map(
        per_device,
        mesh=fine,
        in_specs=placed,
        out_specs=(cells, P("chan"), P(None, "chan")),
        check_vma=False,
    )
```

time: 80.8 us -> 74.4 us (0.921)
  the two profiles are of different devices: /device:TPU:30 before, /device:TPU:1 now
where the time goes in v2:
time: 74.4 us; the launch traced here: 73.9 us
  starting transfers between devices  40.3 us (54%)
  waiting for transfers between devices  11.7 us (16%)
  blocking collectives  11 us (15%)
  Pallas kernels  9.17 us (12%)
  local copies, waits for them, and re-layouts  0.87 us (1%)
  between operations  0.8 us (1%)
    ppermute x2, starting transfers between devices, swap_far(): lax.ppermute(value, GRID, [(i, (i + 1 if i % 2 else i - 1) % n) for i in...  19.3 us
    all_gather x1, blocking collectives, per_device(): got = lax.all_gather(send, 'chan')  11 us
    all_to_all x1, starting transfers between devices, per_device(): cot_all = lax.all_to_all(cots, 'chan', 0, 0).reshape(D, CELLS)  10.3 us
    ppermute x2, waiting for transfers between devices, swap_near(): return lax.ppermute(value, 'xh', [(0, 1), (1, 0)])  7.77 us
    ppermute x2, waiting for transfers between devices, swap_far(): lax.ppermute(value, GRID, [(i, (i + 1 if i % 2 else i - 1) % n) for i in...  3.92 us
    ppermute x2, starting transfers between devices, swap_near(): return lax.ppermute(value, 'xh', [(0, 1), (1, 0)])  3.84 us
    all_to_all x1, starting transfers between devices, per_device(): over_yx = lax.all_to_all(packed, ('y', 'xh'), 0, 0)  3.51 us
    all_to_all x1, starting transfers between devices, per_device(): over_z = lax.all_to_all(again, 'z', 0, 0)  3.35 us
  transfers between devices with their start and end apart: 7, of which 3 were waited for; matrix products, arithmetic and copies ran while one was open for 0% of the time, Pallas kernels for 5%

profile of v2, /device:TPU:1, one launch (start us, length us, event | category | flops | bytes accessed | tf_op | source)
XLA Modules:
  0.0 73.9 jit_solution(16518223727859827776)
XLA Ops:
  0.6 0.0 copy-start.6
  0.6 0.8 %copy-done.6 = bf16[16,8,192]{2,1,0:T(8,128)(2,1)S(1)} copy-done((bf16[16,8,192]{2,1,0:T(8,128)(2,1)S(1)}, bf16[16,8,192]{2,1,0:T(8,128)(2,1)}, u32[]{:S(2)}) %copy-start.6) | copy-done | bytes 49176
  1.5 0.0 copy-start.5
  1.5 0.0 copy-start.2
  1.5 0.0 copy-start.8
  1.5 0.0 copy-start.9
  1.5 0.0 copy-start
  1.5 0.0 copy-start.1
  1.5 0.8 %prep.1 = bf16[4,192,128]{2,1,0:T(8,128)(2,1)} custom-call(bf16[128,192]{1,0:T(8,128)(2,1)S(1)} %bitcast.15), custom_call_target="tpu_custom_call" | custom-call | flops 8000000000 | tf_op jit(solution)/shard_map/prep/pallas_call | solution.py:240
  2.3 10.3 %all-to-all-start = ((bf16[4,192,128]{2,1,0:T(8,128)(2,1)}), bf16[4,192,128]{2,1,0:T(8,128)(2,1)S(1)}, u32[]{:S(2)}, u32[]{:S(2)}) async-start(bf16[4,192,128]{2,1,0:T(8,128)(2,1)} %prep.1), calls=%async_computation | async-start | bytes 393216 | tf_op jit(solution)/shard_map/all_to_all | solution.py:241
  12.6 0.0 copy-done.5
  12.6 10.6 %collective-permute-start.1 = (bf16[128,192]{1,0:T(8,128)(2,1)S(1)}, bf16[128,192]{1,0:T(8,128)(2,1)S(1)}, u32[]{:S(2)}, u32[]{:S(2)}) collective-permute-start(bf16[128,192]{1,0:T(8,128)(2,1)S(1)} %bitcast.12), channel_id=1, source_target_pairs={{0,508},{4,8},{8,4},{12,16},{16,12},{20,24},{24,20},{28,32},{32,28... | collective-permute-start | bytes 147464 | tf_op jit(solution)/shard_map/ppermute | solution.py:230
  23.3 1.9 %collective-permute-start = (bf16[128,192]{1,0:T(8,128)(2,1)S(1)}, bf16[128,192]{1,0:T(8,128)(2,1)S(1)}, u32[]{:S(2)}, u32[]{:S(2)}) collective-permute-start(bf16[128,192]{1,0:T(8,128)(2,1)S(1)} %bitcast.13), channel_id=1, source_target_pairs={{0,4},{4,0},{1,5},{5,1},{2,6},{6,2},{3,7},{7,3},{8,12},{12,8},{9,1... | collective-permute-start | bytes 147464 | tf_op jit(solution)/shard_map/ppermute | solution.py:225
  25.2 0.0 copy-done.2
  25.2 0.0 copy-done.8
  25.2 0.0 copy-done.9
  25.2 0.2 ready.1
  25.5 0.0 all-to-all-done
  25.5 0.0 copy-done
  25.5 0.0 copy-done.1
  25.5 0.0 copy-start.3
  25.5 0.0 copy-start.4
  25.5 1.3 %mlp.1.part = bf16[768,128]{1,0:T(8,128)(2,1)S(1)} custom-call(bf16[768,128]{1,0:T(8,128)(2,1)S(1)} %bitcast.10, f32[768,128]{1,0:T(8,128)S(1)} %get-tuple-element.19.slope, bf16[768,768]{1,0:T(8,128)(2,1)S(1)} %copy-done, bf16[768,768]{1,0:T(8,128)(2,1)S(1)} %copy-done.1), custom_call_target="tpu_custom_call" | custom-call | flops 300000000 | tf_op jit(solution)/shard_map/mlp/pallas_call | solution.py:252
  26.9 0.0 collective-permute-done.1.far
  26.9 2.9 %collective-permute-done.near = bf16[128,192]{1,0:T(8,128)(2,1)S(1)} collective-permute-done((bf16[128,192]{1,0:T(8,128)(2,1)S(1)}, bf16[128,192]{1,0:T(8,128)(2,1)S(1)}, u32[]{:S(2)}, u32[]{:S(2)}) %collective-permute-start) | collective-permute-done | bytes 49184 | tf_op jit(solution)/shard_map/ppermute | solution.py:225
  29.8 0.0 copy-done.3
  29.8 0.0 copy-done.4
  29.8 1.5 %forward.1 = (f32[192,128]{1,0:T(8,128)S(1)}, bf16[976,128]{1,0:T(8,128)(2,1)S(1)}, f32[2,384,128]{2,1,0:T(8,128)S(1)}) custom-call(s32[1]{0:T(128)} %bitcast.place, s32[16,20]{1,0:T(8,128)S(1)} %copy-done.3, f32[16,20]{1,0:T(8,128)S(1)} %copy-done.4, bf16[128,192]{1,0:T(8,128)(2,1)S(1)} %bitcast.14, bf16[128,192]{1,0:T(8,128)(2,1)S(1)} %collective-permute-done.near, ...), custom_call_target="tpu_custom_call" | custom-call | tf_op jit(solution)/shard_map/forward/pallas_call | solution.py:255
  31.3 11.0 %all-gather = bf16[3904,128]{1,0:T(8,128)(2,1)S(1)} all-gather(bf16[976,128]{1,0:T(8,128)(2,1)S(1)} %get-tuple-element.22), channel_id=2, replica_groups=mesh['z'=8,'y'=8,'xh'=2,'chan'=4] {'chan'}, dimensions={0}, use_global_device_ids=true | all-gather | bytes 1249280 | tf_op jit(solution)/shard_map/all_gather | solution.py:263
  42.2 0.0 copy-start.7
  42.2 2.2 %term.1 = (f32[128,192]{1,0:T(8,128)S(1)}, bf16[128,192]{1,0:T(8,128)(2,1)S(1)}, bf16[16,32,128]{2,1,0:T(8,128)(2,1)}) custom-call(s32[1]{0:T(128)} %bitcast.place, s32[16,20]{1,0:T(8,128)S(1)} %copy-done.3, f32[16,20]{1,0:T(8,128)S(1)} %copy-done.4, f32[2,384,128]{2,1,0:T(8,128)S(1)} %get-tuple-element.20.ext, f32[192,128]{1,0:T(8,128)S(1)} %get-tuple-element.21.fwd_t, ...), custom_call_target="tpu_custom_call" | custom-call | tf_op jit(solution)/shard_map/term/pallas_call | solution.py:264
  44.4 3.5 %all-to-all-start.1 = ((bf16[16,32,128]{2,1,0:T(8,128)(2,1)}), bf16[16,32,128]{2,1,0:T(8,128)(2,1)S(1)}, u32[]{:S(2)}, u32[]{:S(2)}) async-start(bf16[16,32,128]{2,1,0:T(8,128)(2,1)} %get-tuple-element.24), calls=%async_computation.1 | async-start | bytes 262144 | tf_op jit(solution)/shard_map/all_to_all | solution.py:272
  47.9 8.7 %collective-permute-start.2 = (bf16[128,192]{1,0:T(8,128)(2,1)S(1)}, bf16[128,192]{1,0:T(8,128)(2,1)S(1)}, u32[]{:S(2)}, u32[]{:S(2)}) collective-permute-start(bf16[128,192]{1,0:T(8,128)(2,1)S(1)} %get-tuple-element.26), channel_id=1, source_target_pairs={{0,508},{4,8},{8,4},{12,16},{16,12},{20,24},{24,20},{28,32},{32,28... | collective-permute-start | bytes 147464 | tf_op jit(solution)/shard_map/ppermute | solution.py:230
  56.6 3.9 %collective-permute-done.2.far = bf16[128,192]{1,0:T(8,128)(2,1)S(1)} collective-permute-done((bf16[128,192]{1,0:T(8,128)(2,1)S(1)}, bf16[128,192]{1,0:T(8,128)(2,1)S(1)}, u32[]{:S(2)}, u32[]{:S(2)}) %collective-permute-start.2) | collective-permute-done | bytes 49184 | tf_op jit(solution)/shard_map/ppermute | solution.py:230
  60.5 0.0 all-to-all-done.1.got
  60.5 0.6 resum.1
  61.1 3.3 %all-to-all-start.2 = ((bf16[8,32,128]{2,1,0:T(8,128)(2,1)}), bf16[8,32,128]{2,1,0:T(8,128)(2,1)S(1)}, u32[]{:S(2)}, u32[]{:S(2)}) async-start(bf16[8,32,128]{2,1,0:T(8,128)(2,1)} %resum.1), calls=%async_computation.2 | async-start | bytes 131072 | tf_op jit(solution)/shard_map/all_to_all | solution.py:276
  64.5 1.9 %collective-permute-start.3 = (bf16[128,192]{1,0:T(8,128)(2,1)S(1)}, bf16[128,192]{1,0:T(8,128)(2,1)S(1)}, u32[]{:S(2)}, u32[]{:S(2)}) collective-permute-start(bf16[128,192]{1,0:T(8,128)(2,1)S(1)} %get-tuple-element.26), channel_id=1, source_target_pairs={{0,4},{4,0},{1,5},{5,1},{2,6},{6,2},{3,7},{7,3},{8,12},{12,8},{9,1... | collective-permute-start | bytes 147464 | tf_op jit(solution)/shard_map/ppermute | solution.py:225
  66.4 4.9 %collective-permute-done.3.near = bf16[128,192]{1,0:T(8,128)(2,1)S(1)} collective-permute-done((bf16[128,192]{1,0:T(8,128)(2,1)S(1)}, bf16[128,192]{1,0:T(8,128)(2,1)S(1)}, u32[]{:S(2)}, u32[]{:S(2)}) %collective-permute-start.3) | collective-permute-done | bytes 49184 | tf_op jit(solution)/shard_map/ppermute | solution.py:225
  71.3 0.0 copy-done.7
  71.3 1.8 %adjoint.1 = bf16[128,192]{1,0:T(8,128)(2,1)} custom-call(s32[1]{0:T(128)} %bitcast.place, s32[16,20]{1,0:T(8,128)S(1)} %copy-done.3, f32[16,20]{1,0:T(8,128)S(1)} %copy-done.4, f32[128,192]{1,0:T(8,128)S(1)} %get-tuple-element.23.own, bf16[128,192]{1,0:T(8,128)(2,1)S(1)} %collective-permute-done.3.near, bf16[128,192]{1,0:T(8,128)(2,1)S(1)} %collective-permute-done.2.far, ...), custom_call_target="tpu_custom_call" | custom-call | bytes 6000000 | tf_op jit(solution)/shard_map/adjoint/pallas_call | solution.py:278
  73.2 0.0 all-to-all-done.2.got
  73.2 0.7 last.1
Async XLA Ops:
  0.6 0.8 %copy-start.6 = (bf16[16,8,192]{2,1,0:T(8,128)(2,1)S(1)}, bf16[16,8,192]{2,1,0:T(8,128)(2,1)}, u32[]{:S(2)}) copy-start(bf16[16,8,192]{2,1,0:T(8,128)(2,1)} %param.10) | copy-start | bytes 147460
  1.5 11.1 %copy-start.5 = (bf16[16,8,192]{2,1,0:T(8,128)(2,1)S(1)}, bf16[16,8,192]{2,1,0:T(8,128)(2,1)}, u32[]{:S(2)}) copy-start(bf16[16,8,192]{2,1,0:T(8,128)(2,1)} %param.9) | copy-start | bytes 147460
  1.5 23.7 %copy-start.2 = (bf16[16,8,768]{2,1,0:T(8,128)(2,1)S(1)}, bf16[16,8,768]{2,1,0:T(8,128)(2,1)}, u32[]{:S(2)}) copy-start(bf16[16,8,768]{2,1,0:T(8,128)(2,1)} %param.11) | copy-start | bytes 589828
  1.5 23.7 %copy-start.8 = (f32[20,192]{1,0:T(8,128)S(1)}, f32[20,192]{1,0:T(8,128)}, u32[]{:S(2)}) copy-start(f32[20,192]{1,0:T(8,128)} %taps.1) | copy-start | bytes 46084
  1.5 23.8 %copy-start.9 = (f32[192]{0:T(256)S(1)}, f32[192]{0:T(256)}, u32[]{:S(2)}) copy-start(f32[192]{0:T(256)} %param.14) | copy-start | bytes 2308
  1.5 24.0 %copy-start = (bf16[768,768]{1,0:T(8,128)(2,1)S(1)}, bf16[768,768]{1,0:T(8,128)(2,1)}, u32[]{:S(2)}) copy-start(bf16[768,768]{1,0:T(8,128)(2,1)} %down.1) | copy-start | bytes 3538948
  1.5 24.0 %copy-start.1 = (bf16[768,768]{1,0:T(8,128)(2,1)S(1)}, bf16[768,768]{1,0:T(8,128)(2,1)}, u32[]{:S(2)}) copy-start(bf16[768,768]{1,0:T(8,128)(2,1)} %up.1) | copy-start | bytes 3538948
  2.3 23.2 %all-to-all-start = ((bf16[4,192,128]{2,1,0:T(8,128)(2,1)}), bf16[4,192,128]{2,1,0:T(8,128)(2,1)S(1)}, u32[]{:S(2)}, u32[]{:S(2)}) async-start(bf16[4,192,128]{2,1,0:T(8,128)(2,1)} %prep.1), calls=%async_computation | async-start | bytes 393216 | tf_op jit(solution)/shard_map/all_to_all | solution.py:241
  12.6 14.3 %collective-permute-start.1 = (bf16[128,192]{1,0:T(8,128)(2,1)S(1)}, bf16[128,192]{1,0:T(8,128)(2,1)S(1)}, u32[]{:S(2)}, u32[]{:S(2)}) collective-permute-start(bf16[128,192]{1,0:T(8,128)(2,1)S(1)} %bitcast.12), channel_id=1, source_target_pairs={{0,508},{4,8},{8,4},{12,16},{16,12},{20,24},{24,20},{28,32},{32,28... | collective-permute-start | bytes 147464 | tf_op jit(solution)/shard_map/ppermute | solution.py:230
  23.3 6.5 %collective-permute-start = (bf16[128,192]{1,0:T(8,128)(2,1)S(1)}, bf16[128,192]{1,0:T(8,128)(2,1)S(1)}, u32[]{:S(2)}, u32[]{:S(2)}) collective-permute-start(bf16[128,192]{1,0:T(8,128)(2,1)S(1)} %bitcast.13), channel_id=1, source_target_pairs={{0,4},{4,0},{1,5},{5,1},{2,6},{6,2},{3,7},{7,3},{8,12},{12,8},{9,1... | collective-permute-start | bytes 147464 | tf_op jit(solution)/shard_map/ppermute | solution.py:225
  25.5 4.3 %copy-start.3 = (s32[16,20]{1,0:T(8,128)S(1)}, s32[16,20]{1,0:T(8,128)}, u32[]{:S(2)}) copy-start(s32[16,20]{1,0:T(8,128)} %offs.5) | copy-start | bytes 3844
  25.5 4.3 %copy-start.4 = (f32[16,20]{1,0:T(8,128)S(1)}, f32[16,20]{1,0:T(8,128)}, u32[]{:S(2)}) copy-start(f32[16,20]{1,0:T(8,128)} %basis.5) | copy-start | bytes 3844
  42.2 29.1 %copy-start.7 = (bf16[16,8,192]{2,1,0:T(8,128)(2,1)S(1)}, bf16[16,8,192]{2,1,0:T(8,128)(2,1)}, u32[]{:S(2)}) copy-start(bf16[16,8,192]{2,1,0:T(8,128)(2,1)} %param.10) | copy-start | bytes 147460
  44.4 16.1 %all-to-all-start.1 = ((bf16[16,32,128]{2,1,0:T(8,128)(2,1)}), bf16[16,32,128]{2,1,0:T(8,128)(2,1)S(1)}, u32[]{:S(2)}, u32[]{:S(2)}) async-start(bf16[16,32,128]{2,1,0:T(8,128)(2,1)} %get-tuple-element.24), calls=%async_computation.1 | async-start | bytes 262144 | tf_op jit(solution)/shard_map/all_to_all | solution.py:272
  47.9 12.6 %collective-permute-start.2 = (bf16[128,192]{1,0:T(8,128)(2,1)S(1)}, bf16[128,192]{1,0:T(8,128)(2,1)S(1)}, u32[]{:S(2)}, u32[]{:S(2)}) collective-permute-start(bf16[128,192]{1,0:T(8,128)(2,1)S(1)} %get-tuple-element.26), channel_id=1, source_target_pairs={{0,508},{4,8},{8,4},{12,16},{16,12},{20,24},{24,20},{28,32},{32,28... | collective-permute-start | bytes 147464 | tf_op jit(solution)/shard_map/ppermute | solution.py:230
  61.1 12.0 %all-to-all-start.2 = ((bf16[8,32,128]{2,1,0:T(8,128)(2,1)}), bf16[8,32,128]{2,1,0:T(8,128)(2,1)S(1)}, u32[]{:S(2)}, u32[]{:S(2)}) async-start(bf16[8,32,128]{2,1,0:T(8,128)(2,1)} %resum.1), calls=%async_computation.2 | async-start | bytes 131072 | tf_op jit(solution)/shard_map/all_to_all | solution.py:276
  64.5 6.8 %collective-permute-start.3 = (bf16[128,192]{1,0:T(8,128)(2,1)S(1)}, bf16[128,192]{1,0:T(8,128)(2,1)S(1)}, u32[]{:S(2)}, u32[]{:S(2)}) collective-permute-start(bf16[128,192]{1,0:T(8,128)(2,1)S(1)} %get-tuple-element.26), channel_id=1, source_target_pairs={{0,4},{4,0},{1,5},{5,1},{2,6},{6,2},{3,7},{7,3},{8,12},{12,8},{9,1... | collective-permute-start | bytes 147464 | tf_op jit(solution)/shard_map/ppermute | solution.py:225

commit v3 on v2

--- a/solution.py
+++ b/solution.py
@@ -63,16 +63,14 @@
     return out
 
 
-def fill_own(ext, ref):
-    v = ref[...].astype(F32)
+def fill_own(ext, v):
     for r in range(ROWS):
         to = pl.ds(EXT * r + LON, LON)
         ext[0, to, :] = v[LON * r : LON * r + LON, :128]
         ext[1, to, : CH - 128] = v[LON * r : LON * r + LON, 128:]
 
 
-def fill_side(ext, ref, start):
-    v = ref[...].astype(F32)
+def fill_side(ext, v, start):
     for r in range(ROWS):
         to = pl.ds(pl.multiple_of(EXT * r + start, LON), LON)
         ext[0, to, :] = v[LON * r : LON * r + LON, :128]
@@ -87,10 +85,13 @@
     fill_side(ext, far, 2 * LON - start)
 
 
-def prep_kernel(cot, out):
-    turned = cot[...].astype(F32).T.astype(BF16)
+def prep_kernel(place, cot, field, out):
+    cot_t = cot[...].astype(F32).T.astype(BF16)
+    field_t = field[...].astype(F32).T.astype(BF16)
+    x_hi = place[0] >> 2
     for i in range(NCHAN):
-        out[i] = turned
+        out[NCHAN * x_hi + i] = cot_t
+        out[NCHAN * (1 - x_hi) + i] = field_t
 
 
 def ready_kernel(pre, gain, taps, slope, gain_t, wide):
@@ -105,14 +106,17 @@
     wide[:, :CH] = taps[...]
 
 
-def mlp_kernel(cot, slope, down, up, out):
-    hidden = jnp.dot(down[...], cot[...], preferred_element_type=F32)
+def mlp_kernel(place, line, slope, down, up, out):
+    cot = line[pl.ds(NCHAN * (place[0] >> 2), NCHAN)].reshape(D, CELLS)
+    hidden = jnp.dot(down[...], cot, preferred_element_type=F32)
     grad = (hidden * slope[...]).astype(BF16)
     out[...] = jnp.dot(up[...], grad, preferred_element_type=F32).astype(BF16)
 
 
-def forward_kernel(place, offs, basis, own, near, far, taps, gain_t, part, fwd_t, send, ext, fwd):
-    fill_ext(ext, place, own, near, far)
+def forward_kernel(place, offs, basis, own, line, far, taps, gain_t, part, fwd_t, send, ext, fwd):
+    x_hi = place[0] >> 2
+    near = line[NCHAN * (1 - x_hi) + (place[0] & 3)].astype(F32).T
+    fill_ext(ext, place, own[...].astype(F32), near, far[...].astype(F32))
     for r in range(ROWS):
         lo = jnp.zeros((LON, 128), F32)
         hi = jnp.zeros((LON, 128), F32)
@@ -175,21 +179,21 @@
     first = rows[0, 0:21, :]
     second = rows[1, 0:HALF, :] + pltpu.roll(rows[1, HALF : 2 * HALF, :], 64, 1)
     value = jnp.concatenate([first, second], axis=0).astype(BF16)
-    for i in range(16):
+    for i in range(8):
         packed[i] = value
 
 
 def resum_kernel(got, out):
     total = got[0].astype(F32)
-    for i in range(1, 16):
+    for i in range(1, 8):
         total += got[i].astype(F32)
     total = total.astype(BF16)
-    for i in range(8):
+    for i in range(16):
         out[i] = total
 
 
 def adjoint_kernel(place, offs, basis, own, near, far, taps, cot, grad, ext, total):
-    fill_ext(ext, place, own, near, far)
+    fill_ext(ext, place, own[...], near[...].astype(F32), far[...].astype(F32))
     for r2 in range(ROWS):
         lo = jnp.zeros((LON, 128), F32)
         hi = jnp.zeros((LON, 128), F32)
@@ -206,7 +210,7 @@
 
 def last_kernel(got, gain_grad, tap_grad):
     value = got[0].astype(F32)
-    for i in range(1, 8):
+    for i in range(1, 16):
         value += got[i].astype(F32)
     value = value * SCALE
     tap_grad[:, :128] = value[0:TAPS]
@@ -237,9 +241,11 @@
     place = lax.axis_index(("xh", "chan")).astype(jnp.int32).reshape(1)
     ext_shape = (2, ROWS * EXT, 128)
 
-    cots = call(prep_kernel, shape((NCHAN, CH, CELLS), BF16), [VMEM], VMEM, [], "prep", flops=8_000_000_000)(cot)
-    cot_all = lax.all_to_all(cots, "chan", 0, 0).reshape(D, CELLS)
-    near, far = swap_near(field), swap_far(field)
+    slots = call(
+        prep_kernel, shape((2 * NCHAN, CH, CELLS), BF16), [SMEM, VMEM, VMEM], VMEM, [], "prep", flops=8_000_000_000, limit=60
+    )(place, cot, field)
+    line = lax.all_to_all(slots, ("xh", "chan"), 0, 0)
+    far = swap_far(field)
     slope, gain_t, taps = call(
         ready_kernel,
         (shape((HID, CELLS)), shape((CH, CELLS)), shape((TAPS, 256))),
@@ -249,8 +255,8 @@
         "ready",
         moved=3_000_000,
     )(pre, gain.reshape(1, CH), tap_weights)
-    part = call(mlp_kernel, shape((D, CELLS), BF16), [VMEM] * 4, VMEM, [], "mlp", flops=300_000_000)(
-        cot_all, slope, w_down, w_up
+    part = call(mlp_kernel, shape((D, CELLS), BF16), [SMEM] + [VMEM] * 4, VMEM, [], "mlp", flops=300_000_000)(
+        place, line, slope, w_down, w_up
     )
     fwd_t, send, ext = call(
         forward_kernel,
@@ -259,21 +265,21 @@
         (VMEM,) * 3,
         [pltpu.VMEM((CELLS, CH), F32)],
         "forward",
-    )(place, lon_offsets, basis, field, near, far, taps, gain_t, part)
+    )(place, lon_offsets, basis, field, line, far, taps, gain_t, part)
     got = lax.all_gather(send, "chan")
     term, term16, packed = call(
         term_kernel,
-        (shape((CELLS, CH)), shape((CELLS, CH), BF16), shape((16, PACK, 128), BF16)),
+        (shape((CELLS, CH)), shape((CELLS, CH), BF16), shape((8, PACK, 128), BF16)),
         [SMEM] * 3 + [VMEM] * 4,
         (VMEM,) * 3,
         [pltpu.VMEM((2, 24, 128), F32)],
         "term",
     )(place, lon_offsets, basis, ext, fwd_t, gain_t, got)
-    over_yx = lax.all_to_all(packed, ("y", "xh"), 0, 0)
-    term_far = swap_far(term16)
-    over_yx, term_far, term_again = lax.optimization_barrier((over_yx, term_far, term16))
-    again = call(resum_kernel, shape((8, PACK, 128), BF16), [VMEM], VMEM, [], "resum")(over_yx)
-    over_z = lax.all_to_all(again, "z", 0, 0)
+    one = lax.all_to_all(packed, "z", 0, 0)
+    term_far = swap_far(term)
+    one, term_again = lax.optimization_barrier((one, term16))
+    again = call(resum_kernel, shape((16, PACK, 128), BF16), [VMEM], VMEM, [], "resum")(one)
+    two = lax.all_to_all(again, ("y", "xh"), 0, 0)
     term_near = swap_near(term_again)
     grad = call(
         adjoint_kernel,
@@ -282,11 +288,11 @@
         VMEM,
         [pltpu.VMEM(ext_shape, F32), pltpu.VMEM((CELLS, CH), F32)],
         "adjoint",
-        moved=6_000_000,
+        flops=2_000_000_000,
     )(place, lon_offsets, basis, term, term_near, term_far, taps, cot)
     gain_grad, tap_grad = call(
         last_kernel, (shape((1, CH)), shape((TAPS, CH))), [VMEM], (VMEM,) * 2, [], "last"
-    )(over_z)
+    )(two)
     return (grad.reshape(ROWS, LON, CH), gain_grad.reshape(CH), tap_grad)
 
 

time: 74.4 us -> 70.5 us (0.948)
  waiting for transfers between devices: 11.7 us -> 3.41 us
  starting transfers between devices: 40.3 us -> 44.2 us
  Pallas kernels: 9.17 us -> 10.3 us
  blocking collectives: 11 us -> 9.88 us
    ppermute x2 -> x1, waiting for transfers between devices: 7.77 us -> 2.07 us  [swap_near(): return lax.ppermute(value, 'xh', [(0, 1), (1, 0)])]
    ppermute x2, waiting for transfers between devices: 3.92 us -> 0.01 us  [swap_far(): lax.ppermute(value, GRID, [(i, (i + 1 if i % 2 else i - 1) % n) for i in...]
    ppermute x2, starting transfers between devices: 19.3 us -> 21.4 us  [swap_far(): lax.ppermute(value, GRID, [(i, (i + 1 if i % 2 else i - 1) % n) for i in...]
    all_to_all x3, waiting for transfers between devices: 0.01 us -> 1.33 us  [the longest x1 1.32 us: per_device(): two = lax.all_to_all(again, ('y', 'xh'), 0, 0)]
    pallas_call x4, Pallas kernels: 4.93 us -> 6.05 us  [the longest x1 2.14 us: per_device(): call(term_kernel, (shape((CELLS, CH)), shape((CELLS, CH), BF16), shape((8...]
    all_gather x1, blocking collectives: 11 us -> 9.88 us  [per_device(): got = lax.all_gather(send, 'chan')]
    ppermute x2 -> x1, starting transfers between devices: 3.84 us -> 4.77 us  [swap_near(): return lax.ppermute(value, 'xh', [(0, 1), (1, 0)])]
    all_to_all x3, starting transfers between devices: 17.2 us -> 18.1 us  [the longest x1 10.2 us: per_device(): line = lax.all_to_all(slots, ('xh', 'chan'), 0, 0)]
  transfers between devices with their start and end apart: 7 -> 6, of which waited for: 3 -> 2; matrix products, arithmetic and copies ran while one was open for 0% -> 0% of each run, Pallas kernels for 5% -> 6%
where the time goes in v3:
time: 70.5 us; the launch traced here: 69.4 us
  starting transfers between devices  44.2 us (63%)
  Pallas kernels  10.3 us (15%)
  blocking collectives  9.88 us (14%)
  waiting for transfers between devices  3.41 us (5%)
  between operations  0.83 us (1%)
  local copies, waits for them, and re-layouts  0.71 us (1%)
    ppermute x2, starting transfers between devices, swap_far(): lax.ppermute(value, GRID, [(i, (i + 1 if i % 2 else i - 1) % n) for i in...  21.4 us
    all_to_all x1, starting transfers between devices, per_device(): line = lax.all_to_all(slots, ('xh', 'chan'), 0, 0)  10.2 us
    all_gather x1, blocking collectives, per_device(): got = lax.all_gather(send, 'chan')  9.88 us
    ppermute x1, starting transfers between devices, swap_near(): return lax.ppermute(value, 'xh', [(0, 1), (1, 0)])  4.77 us
    all_to_all x1, starting transfers between devices, per_device(): two = lax.all_to_all(again, ('y', 'xh'), 0, 0)  4.22 us
    all_to_all x1, starting transfers between devices, per_device(): one = lax.all_to_all(packed, 'z', 0, 0)  3.67 us
    pallas_call x1, Pallas kernels, per_device(): call(term_kernel, (shape((CELLS, CH)), shape((CELLS, CH), BF16), shape((8...  2.14 us
    ppermute x1, waiting for transfers between devices, swap_near(): return lax.ppermute(value, 'xh', [(0, 1), (1, 0)])  2.07 us
  transfers between devices with their start and end apart: 6, of which 2 were waited for; matrix products, arithmetic and copies ran while one was open for 0% of the time, Pallas kernels for 6%

profile of v3, /device:TPU:1, one launch (start us, length us, event | category | flops | bytes accessed | tf_op | source)
XLA Modules:
  0.0 69.4 jit_solution(14888005939656513167)
XLA Ops:
  0.6 0.0 copy-start.3
  0.6 0.0 copy-start.2
  0.7 0.0 copy-start.6
  0.7 0.0 copy-start
  0.7 0.0 copy-start.1
  0.7 1.9 %prep.1 = bf16[8,192,128]{2,1,0:T(8,128)(2,1)} custom-call(s32[1]{0:T(128)} %bitcast.place, bf16[128,192]{1,0:T(8,128)(2,1)} %bitcast.14, bf16[128,192]{1,0:T(8,128)(2,1)} %bitcast.10), custom_call_target="tpu_custom_call" | custom-call | flops 8000000000 | tf_op jit(solution)/shard_map/prep/pallas_call | solution.py:244
  2.6 10.2 %all-to-all-start = ((bf16[8,192,128]{2,1,0:T(8,128)(2,1)}), bf16[8,192,128]{2,1,0:T(8,128)(2,1)S(1)}, u32[]{:S(2)}, u32[]{:S(2)}) async-start(bf16[8,192,128]{2,1,0:T(8,128)(2,1)} %prep.1), calls=%async_computation | async-start | bytes 786432 | tf_op jit(solution)/shard_map/all_to_all | solution.py:247
  12.8 0.0 copy-done.3
  12.8 11.7 %collective-permute-start = (bf16[128,192]{1,0:T(8,128)(2,1)S(1)}, bf16[128,192]{1,0:T(8,128)(2,1)}, u32[]{:S(2)}, u32[]{:S(2)}) collective-permute-start(bf16[128,192]{1,0:T(8,128)(2,1)S(1)} %bitcast.11), channel_id=1, source_target_pairs={{0,508},{4,8},{8,4},{12,16},{16,12},{20,24},{24,20},{28,32},{32,28... | collective-permute-start | bytes 147464 | tf_op jit(solution)/shard_map/ppermute | solution.py:234
  24.6 0.0 copy-done.2
  24.6 0.0 copy-done.6
  24.6 0.0 copy-start.7
  24.6 0.7 copy-done.7
  25.3 0.2 ready.1
  25.5 0.0 all-to-all-done.line
  25.5 0.0 copy-done
  25.5 0.0 copy-done.1
  25.6 0.0 copy-start.4
  25.6 0.0 copy-start.5
  25.6 1.3 %mlp.1.part = bf16[768,128]{1,0:T(8,128)(2,1)S(1)} custom-call(s32[1]{0:T(128)} %bitcast.place, bf16[8,192,128]{2,1,0:T(8,128)(2,1)S(1)} %all-to-all-done.line, f32[768,128]{1,0:T(8,128)S(1)} %get-tuple-element.18.slope, bf16[768,768]{1,0:T(8,128)(2,1)S(1)} %copy-done, bf16[768,768]{1,0:T(8,128)(2,1)S(1)} %copy-done.1), custom_call_target="tpu_custom_call" | custom-call | flops 300000000 | tf_op jit(solution)/shard_map/mlp/pallas_call | solution.py:258
  26.9 0.0 collective-permute-done.far
  26.9 0.0 copy-done.4
  26.9 0.0 copy-done.5
  27.0 1.5 %forward.1 = (f32[192,128]{1,0:T(8,128)S(1)}, bf16[976,128]{1,0:T(8,128)(2,1)S(1)}, f32[2,384,128]{2,1,0:T(8,128)S(1)}) custom-call(s32[1]{0:T(128)} %bitcast.place, s32[16,20]{1,0:T(8,128)S(1)} %copy-done.4, f32[16,20]{1,0:T(8,128)S(1)} %copy-done.5, bf16[128,192]{1,0:T(8,128)(2,1)S(1)} %bitcast.12, bf16[8,192,128]{2,1,0:T(8,128)(2,1)S(1)} %all-to-all-done.line, ...), custom_call_target="tpu_custom_call" | custom-call | tf_op jit(solution)/shard_map/forward/pallas_call | solution.py:261
  28.5 9.9 %all-gather = bf16[3904,128]{1,0:T(8,128)(2,1)S(1)} all-gather(bf16[976,128]{1,0:T(8,128)(2,1)S(1)} %get-tuple-element.21), channel_id=2, replica_groups=mesh['z'=8,'y'=8,'xh'=2,'chan'=4] {'chan'}, dimensions={0}, use_global_device_ids=true | all-gather | bytes 1249280 | tf_op jit(solution)/shard_map/all_gather | solution.py:269
  38.3 0.0 copy-start.8
  38.3 2.1 %term.1 = (f32[128,192]{1,0:T(8,128)S(1)}, bf16[128,192]{1,0:T(8,128)(2,1)S(1)}, bf16[8,32,128]{2,1,0:T(8,128)(2,1)}) custom-call(s32[1]{0:T(128)} %bitcast.place, s32[16,20]{1,0:T(8,128)S(1)} %copy-done.4, f32[16,20]{1,0:T(8,128)S(1)} %copy-done.5, f32[2,384,128]{2,1,0:T(8,128)S(1)} %get-tuple-element.19.ext, f32[192,128]{1,0:T(8,128)S(1)} %get-tuple-element.20.fwd_t, ...), custom_call_target="tpu_custom_call" | custom-call | tf_op jit(solution)/shard_map/term/pallas_call | solution.py:270
  40.5 3.7 %all-to-all-start.1 = ((bf16[8,32,128]{2,1,0:T(8,128)(2,1)}), bf16[8,32,128]{2,1,0:T(8,128)(2,1)S(1)}, u32[]{:S(2)}, u32[]{:S(2)}) async-start(bf16[8,32,128]{2,1,0:T(8,128)(2,1)} %get-tuple-element.23), calls=%async_computation.1 | async-start | bytes 131072 | tf_op jit(solution)/shard_map/all_to_all | solution.py:278
  44.1 9.6 %collective-permute-start.2 = (f32[128,192]{1,0:T(8,128)S(1)}, f32[128,192]{1,0:T(8,128)S(1)}, u32[]{:S(2)}, u32[]{:S(2)}) collective-permute-start(f32[128,192]{1,0:T(8,128)S(1)} %get-tuple-element.22.own), channel_id=1, source_target_pairs={{0,508},{4,8},{8,4},{12,16},{16,12},{20,24},{24,20},{28,32},{32,28... | collective-permute-start | bytes 294920 | tf_op jit(solution)/shard_map/ppermute | solution.py:234
  53.8 0.0 all-to-all-done.1.got
  53.8 0.7 resum.1
  54.5 4.2 %all-to-all-start.2 = ((bf16[16,32,128]{2,1,0:T(8,128)(2,1)}), bf16[16,32,128]{2,1,0:T(8,128)(2,1)S(1)}, u32[]{:S(2)}, u32[]{:S(2)}) async-start(bf16[16,32,128]{2,1,0:T(8,128)(2,1)} %resum.1), calls=%async_computation.2 | async-start | bytes 262144 | tf_op jit(solution)/shard_map/all_to_all | solution.py:282
  58.7 4.8 %collective-permute-start.1 = (bf16[128,192]{1,0:T(8,128)(2,1)S(1)}, bf16[128,192]{1,0:T(8,128)(2,1)S(1)}, u32[]{:S(2)}, u32[]{:S(2)}) collective-permute-start(bf16[128,192]{1,0:T(8,128)(2,1)S(1)} %get-tuple-element.25), channel_id=1, source_target_pairs={{0,4},{4,0},{1,5},{5,1},{2,6},{6,2},{3,7},{7,3},{8,12},{12,8},{9,1... | collective-permute-start | bytes 147464 | tf_op jit(solution)/shard_map/ppermute | solution.py:229
  63.5 0.0 collective-permute-done.2.far
  63.5 2.1 %collective-permute-done.1.near = bf16[128,192]{1,0:T(8,128)(2,1)S(1)} collective-permute-done((bf16[128,192]{1,0:T(8,128)(2,1)S(1)}, bf16[128,192]{1,0:T(8,128)(2,1)S(1)}, u32[]{:S(2)}, u32[]{:S(2)}) %collective-permute-start.1) | collective-permute-done | bytes 49184 | tf_op jit(solution)/shard_map/ppermute | solution.py:229
  65.5 0.0 copy-done.8
  65.5 1.8 %adjoint.1 = bf16[128,192]{1,0:T(8,128)(2,1)} custom-call(s32[1]{0:T(128)} %bitcast.place, s32[16,20]{1,0:T(8,128)S(1)} %copy-done.4, f32[16,20]{1,0:T(8,128)S(1)} %copy-done.5, f32[128,192]{1,0:T(8,128)S(1)} %get-tuple-element.22.own, bf16[128,192]{1,0:T(8,128)(2,1)S(1)} %collective-permute-done.1.near, f32[128,192]{1,0:T(8,128)S(1)} %collective-permute-done.2.far, ...), custom_call_target="tpu_custom_call" | custom-call | flops 2000000000 | tf_op jit(solution)/shard_map/adjoint/pallas_call | solution.py:284
  67.4 1.3 %all-to-all-done.2.got = bf16[16,32,128]{2,1,0:T(8,128)(2,1)S(1)} async-done(((bf16[16,32,128]{2,1,0:T(8,128)(2,1)}), bf16[16,32,128]{2,1,0:T(8,128)(2,1)S(1)}, u32[]{:S(2)}, u32[]{:S(2)}) %all-to-all-start.2) | async-done | bytes 131104 | tf_op jit(solution)/shard_map/all_to_all | solution.py:282
  68.7 0.7 %last.1 = (f32[1,192]{1,0:T(1,128)}, f32[20,192]{1,0:T(8,128)}) custom-call(bf16[16,32,128]{2,1,0:T(8,128)(2,1)S(1)} %all-to-all-done.2.got), custom_call_target="tpu_custom_call" | custom-call | tf_op jit(solution)/shard_map/last/pallas_call | solution.py:293
Async XLA Ops:
  0.6 12.2 %copy-start.3 = (bf16[16,8,192]{2,1,0:T(8,128)(2,1)S(1)}, bf16[16,8,192]{2,1,0:T(8,128)(2,1)}, u32[]{:S(2)}) copy-start(bf16[16,8,192]{2,1,0:T(8,128)(2,1)} %param.9) | copy-start | bytes 147460
  0.6 23.9 %copy-start.2 = (bf16[16,8,768]{2,1,0:T(8,128)(2,1)S(1)}, bf16[16,8,768]{2,1,0:T(8,128)(2,1)}, u32[]{:S(2)}) copy-start(bf16[16,8,768]{2,1,0:T(8,128)(2,1)} %param.11) | copy-start | bytes 589828
  0.7 23.9 %copy-start.6 = (f32[20,192]{1,0:T(8,128)S(1)}, f32[20,192]{1,0:T(8,128)}, u32[]{:S(2)}) copy-start(f32[20,192]{1,0:T(8,128)} %taps.1) | copy-start | bytes 46084
  0.7 24.9 %copy-start = (bf16[768,768]{1,0:T(8,128)(2,1)S(1)}, bf16[768,768]{1,0:T(8,128)(2,1)}, u32[]{:S(2)}) copy-start(bf16[768,768]{1,0:T(8,128)(2,1)} %down.1) | copy-start | bytes 3538948
  0.7 24.9 %copy-start.1 = (bf16[768,768]{1,0:T(8,128)(2,1)S(1)}, bf16[768,768]{1,0:T(8,128)(2,1)}, u32[]{:S(2)}) copy-start(bf16[768,768]{1,0:T(8,128)(2,1)} %up.1) | copy-start | bytes 3538948
  2.6 22.9 %all-to-all-start = ((bf16[8,192,128]{2,1,0:T(8,128)(2,1)}), bf16[8,192,128]{2,1,0:T(8,128)(2,1)S(1)}, u32[]{:S(2)}, u32[]{:S(2)}) async-start(bf16[8,192,128]{2,1,0:T(8,128)(2,1)} %prep.1), calls=%async_computation | async-start | bytes 786432 | tf_op jit(solution)/shard_map/all_to_all | solution.py:247
  12.8 14.1 %collective-permute-start = (bf16[128,192]{1,0:T(8,128)(2,1)S(1)}, bf16[128,192]{1,0:T(8,128)(2,1)}, u32[]{:S(2)}, u32[]{:S(2)}) collective-permute-start(bf16[128,192]{1,0:T(8,128)(2,1)S(1)} %bitcast.11), channel_id=1, source_target_pairs={{0,508},{4,8},{8,4},{12,16},{16,12},{20,24},{24,20},{28,32},{32,28... | collective-permute-start | bytes 147464 | tf_op jit(solution)/shard_map/ppermute | solution.py:234
  24.6 0.7 copy-start.7
  25.6 1.4 %copy-start.4 = (s32[16,20]{1,0:T(8,128)S(1)}, s32[16,20]{1,0:T(8,128)}, u32[]{:S(2)}) copy-start(s32[16,20]{1,0:T(8,128)} %offs.5) | copy-start | bytes 3844
  25.6 1.4 %copy-start.5 = (f32[16,20]{1,0:T(8,128)S(1)}, f32[16,20]{1,0:T(8,128)}, u32[]{:S(2)}) copy-start(f32[16,20]{1,0:T(8,128)} %basis.5) | copy-start | bytes 3844
  38.3 27.2 %copy-start.8 = (bf16[16,8,192]{2,1,0:T(8,128)(2,1)S(1)}, bf16[16,8,192]{2,1,0:T(8,128)(2,1)}, u32[]{:S(2)}) copy-start(bf16[16,8,192]{2,1,0:T(8,128)(2,1)} %param.10) | copy-start | bytes 147460
  40.5 13.3 %all-to-all-start.1 = ((bf16[8,32,128]{2,1,0:T(8,128)(2,1)}), bf16[8,32,128]{2,1,0:T(8,128)(2,1)S(1)}, u32[]{:S(2)}, u32[]{:S(2)}) async-start(bf16[8,32,128]{2,1,0:T(8,128)(2,1)} %get-tuple-element.23), calls=%async_computation.1 | async-start | bytes 131072 | tf_op jit(solution)/shard_map/all_to_all | solution.py:278
  44.1 19.3 %collective-permute-start.2 = (f32[128,192]{1,0:T(8,128)S(1)}, f32[128,192]{1,0:T(8,128)S(1)}, u32[]{:S(2)}, u32[]{:S(2)}) collective-permute-start(f32[128,192]{1,0:T(8,128)S(1)} %get-tuple-element.22.own), channel_id=1, source_target_pairs={{0,508},{4,8},{8,4},{12,16},{16,12},{20,24},{24,20},{28,32},{32,28... | collective-permute-start | bytes 294920 | tf_op jit(solution)/shard_map/ppermute | solution.py:234
  54.5 14.3 %all-to-all-start.2 = ((bf16[16,32,128]{2,1,0:T(8,128)(2,1)}), bf16[16,32,128]{2,1,0:T(8,128)(2,1)S(1)}, u32[]{:S(2)}, u32[]{:S(2)}) async-start(bf16[16,32,128]{2,1,0:T(8,128)(2,1)} %resum.1), calls=%async_computation.2 | async-start | bytes 262144 | tf_op jit(solution)/shard_map/all_to_all | solution.py:282
  58.7 6.9 %collective-permute-start.1 = (bf16[128,192]{1,0:T(8,128)(2,1)S(1)}, bf16[128,192]{1,0:T(8,128)(2,1)S(1)}, u32[]{:S(2)}, u32[]{:S(2)}) collective-permute-start(bf16[128,192]{1,0:T(8,128)(2,1)S(1)} %get-tuple-element.25), channel_id=1, source_target_pairs={{0,4},{4,0},{1,5},{5,1},{2,6},{6,2},{3,7},{7,3},{8,12},{12,8},{9,1... | collective-permute-start | bytes 147464 | tf_op jit(solution)/shard_map/ppermute | solution.py:229

commit v4 on v3

--- a/solution.py
+++ b/solution.py
@@ -100,7 +100,7 @@
         0.5 * (1.0 + lax.erf(v * INV_SQRT_TWO))
         + v * jnp.exp(-0.5 * v * v) * INV_SQRT_TWO_PI
     )
-    slope[...] = s.T
+    slope[...] = s
     gain_t[...] = jnp.broadcast_to(gain[...], (CELLS, CH)).T
     wide[...] = jnp.zeros((TAPS, 256), F32)
     wide[:, :CH] = taps[...]
@@ -108,9 +108,11 @@
 
 def mlp_kernel(place, line, slope, down, up, out):
     cot = line[pl.ds(NCHAN * (place[0] >> 2), NCHAN)].reshape(D, CELLS)
-    hidden = jnp.dot(down[...], cot, preferred_element_type=F32)
+    hidden = lax.dot_general(
+        cot.astype(F32).T.astype(BF16), down[...], NT, preferred_element_type=F32
+    )
     grad = (hidden * slope[...]).astype(BF16)
-    out[...] = jnp.dot(up[...], grad, preferred_element_type=F32).astype(BF16)
+    out[...] = lax.dot_general(grad, up[...], NT, preferred_element_type=F32).T.astype(BF16)
 
 
 def forward_kernel(place, offs, basis, own, line, far, taps, gain_t, part, fwd_t, send, ext, fwd):
@@ -248,7 +250,7 @@
     far = swap_far(field)
     slope, gain_t, taps = call(
         ready_kernel,
-        (shape((HID, CELLS)), shape((CH, CELLS)), shape((TAPS, 256))),
+        (shape((CELLS, HID)), shape((CH, CELLS)), shape((TAPS, 256))),
         [VMEM] * 3,
         (VMEM,) * 3,
         [],

time: 70.5 us -> 70.5 us (level)
  transfers between devices with their start and end apart: 6 -> 6, of which waited for: 2 -> 3; matrix products, arithmetic and copies ran while one was open for 0% -> 0% of each run, Pallas kernels for 6% -> 5%
where the time goes in v4:
time: 70.5 us; the launch traced here: 69.4 us
  starting transfers between devices  44.4 us (63%)
  Pallas kernels  9.99 us (14%)
  blocking collectives  9.88 us (14%)
  waiting for transfers between devices  3.66 us (5%)
  between operations  0.81 us (1%)
  local copies, waits for them, and re-layouts  0.71 us (1%)
    ppermute x2, starting transfers between devices, swap_far(): lax.ppermute(value, GRID, [(i, (i + 1 if i % 2 else i - 1) % n) for i in...  21.4 us
    all_to_all x1, starting transfers between devices, per_device(): line = lax.all_to_all(slots, ('xh', 'chan'), 0, 0)  10.2 us
    all_gather x1, blocking collectives, per_device(): got = lax.all_gather(send, 'chan')  9.88 us
    ppermute x1, starting transfers between devices, swap_near(): return lax.ppermute(value, 'xh', [(0, 1), (1, 0)])  4.77 us
    all_to_all x1, starting transfers between devices, per_device(): two = lax.all_to_all(again, ('y', 'xh'), 0, 0)  4.22 us
    all_to_all x1, starting transfers between devices, per_device(): one = lax.all_to_all(packed, 'z', 0, 0)  3.79 us
    pallas_call x1, Pallas kernels, per_device(): call(term_kernel, (shape((CELLS, CH)), shape((CELLS, CH), BF16), shape((8...  2.14 us
    ppermute x1, waiting for transfers between devices, swap_near(): return lax.ppermute(value, 'xh', [(0, 1), (1, 0)])  2.07 us
  transfers between devices with their start and end apart: 6, of which 3 were waited for; matrix products, arithmetic and copies ran while one was open for 0% of the time, Pallas kernels for 5%

profile of v4, /device:TPU:1, one launch (start us, length us, event | category | flops | bytes accessed | tf_op | source)
XLA Modules:
  0.0 69.4 jit_solution(14195236408336428403)
XLA Ops:
  0.6 0.0 copy-start.3
  0.6 0.0 copy-start.2
  0.7 0.0 copy-start.6
  0.7 0.0 copy-start
  0.7 0.0 copy-start.1
  0.7 1.9 %prep.1 = bf16[8,192,128]{2,1,0:T(8,128)(2,1)} custom-call(s32[1]{0:T(128)} %bitcast.place, bf16[128,192]{1,0:T(8,128)(2,1)} %bitcast.14, bf16[128,192]{1,0:T(8,128)(2,1)} %bitcast.10), custom_call_target="tpu_custom_call" | custom-call | flops 8000000000 | tf_op jit(solution)/shard_map/prep/pallas_call | solution.py:246
  2.6 10.2 %all-to-all-start = ((bf16[8,192,128]{2,1,0:T(8,128)(2,1)}), bf16[8,192,128]{2,1,0:T(8,128)(2,1)S(1)}, u32[]{:S(2)}, u32[]{:S(2)}) async-start(bf16[8,192,128]{2,1,0:T(8,128)(2,1)} %prep.1), calls=%async_computation | async-start | bytes 786432 | tf_op jit(solution)/shard_map/all_to_all | solution.py:249
  12.8 0.0 copy-done.3
  12.8 11.7 %collective-permute-start = (bf16[128,192]{1,0:T(8,128)(2,1)S(1)}, bf16[128,192]{1,0:T(8,128)(2,1)}, u32[]{:S(2)}, u32[]{:S(2)}) collective-permute-start(bf16[128,192]{1,0:T(8,128)(2,1)S(1)} %bitcast.11), channel_id=1, source_target_pairs={{0,508},{4,8},{8,4},{12,16},{16,12},{20,24},{24,20},{28,32},{32,28... | collective-permute-start | bytes 147464 | tf_op jit(solution)/shard_map/ppermute | solution.py:236
  24.6 0.0 copy-done.2
  24.6 0.0 copy-done.6
  24.6 0.0 copy-start.7
  24.6 0.7 copy-done.7
  25.3 0.2 ready.1
  25.5 0.0 all-to-all-done.line
  25.5 0.0 copy-done
  25.5 0.0 copy-done.1
  25.5 0.0 copy-start.4
  25.5 0.0 copy-start.5
  25.6 1.0 %mlp.1.part = bf16[768,128]{1,0:T(8,128)(2,1)S(1)} custom-call(s32[1]{0:T(128)} %bitcast.place, bf16[8,192,128]{2,1,0:T(8,128)(2,1)S(1)} %all-to-all-done.line, f32[128,768]{1,0:T(8,128)S(1)} %get-tuple-element.18.slope, bf16[768,768]{1,0:T(8,128)(2,1)S(1)} %copy-done, bf16[768,768]{1,0:T(8,128)(2,1)S(1)} %copy-done.1), custom_call_target="tpu_custom_call" | custom-call | flops 300000000 | tf_op jit(solution)/shard_map/mlp/pallas_call | solution.py:260
  26.6 0.3 collective-permute-done.far
  26.8 0.0 copy-done.4
  26.8 0.0 copy-done.5
  26.8 1.5 %forward.1 = (f32[192,128]{1,0:T(8,128)S(1)}, bf16[976,128]{1,0:T(8,128)(2,1)S(1)}, f32[2,384,128]{2,1,0:T(8,128)S(1)}) custom-call(s32[1]{0:T(128)} %bitcast.place, s32[16,20]{1,0:T(8,128)S(1)} %copy-done.4, f32[16,20]{1,0:T(8,128)S(1)} %copy-done.5, bf16[128,192]{1,0:T(8,128)(2,1)S(1)} %bitcast.12, bf16[8,192,128]{2,1,0:T(8,128)(2,1)S(1)} %all-to-all-done.line, ...), custom_call_target="tpu_custom_call" | custom-call | tf_op jit(solution)/shard_map/forward/pallas_call | solution.py:263
  28.3 9.9 %all-gather = bf16[3904,128]{1,0:T(8,128)(2,1)S(1)} all-gather(bf16[976,128]{1,0:T(8,128)(2,1)S(1)} %get-tuple-element.21), channel_id=2, replica_groups=mesh['z'=8,'y'=8,'xh'=2,'chan'=4] {'chan'}, dimensions={0}, use_global_device_ids=true | all-gather | bytes 1249280 | tf_op jit(solution)/shard_map/all_gather | solution.py:271
  38.2 0.0 copy-start.8
  38.2 2.1 %term.1 = (f32[128,192]{1,0:T(8,128)S(1)}, bf16[128,192]{1,0:T(8,128)(2,1)S(1)}, bf16[8,32,128]{2,1,0:T(8,128)(2,1)}) custom-call(s32[1]{0:T(128)} %bitcast.place, s32[16,20]{1,0:T(8,128)S(1)} %copy-done.4, f32[16,20]{1,0:T(8,128)S(1)} %copy-done.5, f32[2,384,128]{2,1,0:T(8,128)S(1)} %get-tuple-element.19.ext, f32[192,128]{1,0:T(8,128)S(1)} %get-tuple-element.20.fwd_t, ...), custom_call_target="tpu_custom_call" | custom-call | tf_op jit(solution)/shard_map/term/pallas_call | solution.py:272
  40.4 3.8 %all-to-all-start.1 = ((bf16[8,32,128]{2,1,0:T(8,128)(2,1)}), bf16[8,32,128]{2,1,0:T(8,128)(2,1)S(1)}, u32[]{:S(2)}, u32[]{:S(2)}) async-start(bf16[8,32,128]{2,1,0:T(8,128)(2,1)} %get-tuple-element.23), calls=%async_computation.1 | async-start | bytes 131072 | tf_op jit(solution)/shard_map/all_to_all | solution.py:280
  44.1 9.6 %collective-permute-start.2 = (f32[128,192]{1,0:T(8,128)S(1)}, f32[128,192]{1,0:T(8,128)S(1)}, u32[]{:S(2)}, u32[]{:S(2)}) collective-permute-start(f32[128,192]{1,0:T(8,128)S(1)} %get-tuple-element.22.own), channel_id=1, source_target_pairs={{0,508},{4,8},{8,4},{12,16},{16,12},{20,24},{24,20},{28,32},{32,28... | collective-permute-start | bytes 294920 | tf_op jit(solution)/shard_map/ppermute | solution.py:236
  53.8 0.0 all-to-all-done.1.got
  53.8 0.7 resum.1
  54.5 4.2 %all-to-all-start.2 = ((bf16[16,32,128]{2,1,0:T(8,128)(2,1)}), bf16[16,32,128]{2,1,0:T(8,128)(2,1)S(1)}, u32[]{:S(2)}, u32[]{:S(2)}) async-start(bf16[16,32,128]{2,1,0:T(8,128)(2,1)} %resum.1), calls=%async_computation.2 | async-start | bytes 262144 | tf_op jit(solution)/shard_map/all_to_all | solution.py:284
  58.7 4.8 %collective-permute-start.1 = (bf16[128,192]{1,0:T(8,128)(2,1)S(1)}, bf16[128,192]{1,0:T(8,128)(2,1)S(1)}, u32[]{:S(2)}, u32[]{:S(2)}) collective-permute-start(bf16[128,192]{1,0:T(8,128)(2,1)S(1)} %get-tuple-element.25), channel_id=1, source_target_pairs={{0,4},{4,0},{1,5},{5,1},{2,6},{6,2},{3,7},{7,3},{8,12},{12,8},{9,1... | collective-permute-start | bytes 147464 | tf_op jit(solution)/shard_map/ppermute | solution.py:231
  63.5 0.0 collective-permute-done.2.far
  63.5 2.1 %collective-permute-done.1.near = bf16[128,192]{1,0:T(8,128)(2,1)S(1)} collective-permute-done((bf16[128,192]{1,0:T(8,128)(2,1)S(1)}, bf16[128,192]{1,0:T(8,128)(2,1)S(1)}, u32[]{:S(2)}, u32[]{:S(2)}) %collective-permute-start.1) | collective-permute-done | bytes 49184 | tf_op jit(solution)/shard_map/ppermute | solution.py:231
  65.5 0.0 copy-done.8
  65.5 1.8 %adjoint.1 = bf16[128,192]{1,0:T(8,128)(2,1)} custom-call(s32[1]{0:T(128)} %bitcast.place, s32[16,20]{1,0:T(8,128)S(1)} %copy-done.4, f32[16,20]{1,0:T(8,128)S(1)} %copy-done.5, f32[128,192]{1,0:T(8,128)S(1)} %get-tuple-element.22.own, bf16[128,192]{1,0:T(8,128)(2,1)S(1)} %collective-permute-done.1.near, f32[128,192]{1,0:T(8,128)S(1)} %collective-permute-done.2.far, ...), custom_call_target="tpu_custom_call" | custom-call | flops 2000000000 | tf_op jit(solution)/shard_map/adjoint/pallas_call | solution.py:286
  67.4 1.3 %all-to-all-done.2.got = bf16[16,32,128]{2,1,0:T(8,128)(2,1)S(1)} async-done(((bf16[16,32,128]{2,1,0:T(8,128)(2,1)}), bf16[16,32,128]{2,1,0:T(8,128)(2,1)S(1)}, u32[]{:S(2)}, u32[]{:S(2)}) %all-to-all-start.2) | async-done | bytes 131104 | tf_op jit(solution)/shard_map/all_to_all | solution.py:284
  68.7 0.7 %last.1 = (f32[1,192]{1,0:T(1,128)}, f32[20,192]{1,0:T(8,128)}) custom-call(bf16[16,32,128]{2,1,0:T(8,128)(2,1)S(1)} %all-to-all-done.2.got), custom_call_target="tpu_custom_call" | custom-call | tf_op jit(solution)/shard_map/last/pallas_call | solution.py:295
Async XLA Ops:
  0.6 12.2 %copy-start.3 = (bf16[16,8,192]{2,1,0:T(8,128)(2,1)S(1)}, bf16[16,8,192]{2,1,0:T(8,128)(2,1)}, u32[]{:S(2)}) copy-start(bf16[16,8,192]{2,1,0:T(8,128)(2,1)} %param.9) | copy-start | bytes 147460
  0.6 23.9 %copy-start.2 = (bf16[16,8,768]{2,1,0:T(8,128)(2,1)S(1)}, bf16[16,8,768]{2,1,0:T(8,128)(2,1)}, u32[]{:S(2)}) copy-start(bf16[16,8,768]{2,1,0:T(8,128)(2,1)} %param.11) | copy-start | bytes 589828
  0.7 23.9 %copy-start.6 = (f32[20,192]{1,0:T(8,128)S(1)}, f32[20,192]{1,0:T(8,128)}, u32[]{:S(2)}) copy-start(f32[20,192]{1,0:T(8,128)} %taps.1) | copy-start | bytes 46084
  0.7 24.8 %copy-start = (bf16[768,768]{1,0:T(8,128)(2,1)S(1)}, bf16[768,768]{1,0:T(8,128)(2,1)}, u32[]{:S(2)}) copy-start(bf16[768,768]{1,0:T(8,128)(2,1)} %down.1) | copy-start | bytes 3538948
  0.7 24.8 %copy-start.1 = (bf16[768,768]{1,0:T(8,128)(2,1)S(1)}, bf16[768,768]{1,0:T(8,128)(2,1)}, u32[]{:S(2)}) copy-start(bf16[768,768]{1,0:T(8,128)(2,1)} %up.1) | copy-start | bytes 3538948
  2.6 22.9 %all-to-all-start = ((bf16[8,192,128]{2,1,0:T(8,128)(2,1)}), bf16[8,192,128]{2,1,0:T(8,128)(2,1)S(1)}, u32[]{:S(2)}, u32[]{:S(2)}) async-start(bf16[8,192,128]{2,1,0:T(8,128)(2,1)} %prep.1), calls=%async_computation | async-start | bytes 786432 | tf_op jit(solution)/shard_map/all_to_all | solution.py:249
  12.8 14.0 %collective-permute-start = (bf16[128,192]{1,0:T(8,128)(2,1)S(1)}, bf16[128,192]{1,0:T(8,128)(2,1)}, u32[]{:S(2)}, u32[]{:S(2)}) collective-permute-start(bf16[128,192]{1,0:T(8,128)(2,1)S(1)} %bitcast.11), channel_id=1, source_target_pairs={{0,508},{4,8},{8,4},{12,16},{16,12},{20,24},{24,20},{28,32},{32,28... | collective-permute-start | bytes 147464 | tf_op jit(solution)/shard_map/ppermute | solution.py:236
  24.6 0.7 copy-start.7
  25.5 1.3 %copy-start.4 = (s32[16,20]{1,0:T(8,128)S(1)}, s32[16,20]{1,0:T(8,128)}, u32[]{:S(2)}) copy-start(s32[16,20]{1,0:T(8,128)} %offs.5) | copy-start | bytes 3844
  25.5 1.3 %copy-start.5 = (f32[16,20]{1,0:T(8,128)S(1)}, f32[16,20]{1,0:T(8,128)}, u32[]{:S(2)}) copy-start(f32[16,20]{1,0:T(8,128)} %basis.5) | copy-start | bytes 3844
  38.2 27.3 %copy-start.8 = (bf16[16,8,192]{2,1,0:T(8,128)(2,1)S(1)}, bf16[16,8,192]{2,1,0:T(8,128)(2,1)}, u32[]{:S(2)}) copy-start(bf16[16,8,192]{2,1,0:T(8,128)(2,1)} %param.10) | copy-start | bytes 147460
  40.4 13.4 %all-to-all-start.1 = ((bf16[8,32,128]{2,1,0:T(8,128)(2,1)}), bf16[8,32,128]{2,1,0:T(8,128)(2,1)S(1)}, u32[]{:S(2)}, u32[]{:S(2)}) async-start(bf16[8,32,128]{2,1,0:T(8,128)(2,1)} %get-tuple-element.23), calls=%async_computation.1 | async-start | bytes 131072 | tf_op jit(solution)/shard_map/all_to_all | solution.py:280
  44.1 19.3 %collective-permute-start.2 = (f32[128,192]{1,0:T(8,128)S(1)}, f32[128,192]{1,0:T(8,128)S(1)}, u32[]{:S(2)}, u32[]{:S(2)}) collective-permute-start(f32[128,192]{1,0:T(8,128)S(1)} %get-tuple-element.22.own), channel_id=1, source_target_pairs={{0,508},{4,8},{8,4},{12,16},{16,12},{20,24},{24,20},{28,32},{32,28... | collective-permute-start | bytes 294920 | tf_op jit(solution)/shard_map/ppermute | solution.py:236
  54.5 14.3 %all-to-all-start.2 = ((bf16[16,32,128]{2,1,0:T(8,128)(2,1)}), bf16[16,32,128]{2,1,0:T(8,128)(2,1)S(1)}, u32[]{:S(2)}, u32[]{:S(2)}) async-start(bf16[16,32,128]{2,1,0:T(8,128)(2,1)} %resum.1), calls=%async_computation.2 | async-start | bytes 262144 | tf_op jit(solution)/shard_map/all_to_all | solution.py:284
  58.7 6.9 %collective-permute-start.1 = (bf16[128,192]{1,0:T(8,128)(2,1)S(1)}, bf16[128,192]{1,0:T(8,128)(2,1)S(1)}, u32[]{:S(2)}, u32[]{:S(2)}) collective-permute-start(bf16[128,192]{1,0:T(8,128)(2,1)S(1)} %get-tuple-element.25), channel_id=1, source_target_pairs={{0,4},{4,0},{1,5},{5,1},{2,6},{6,2},{3,7},{7,3},{8,12},{12,8},{9,1... | collective-permute-start | bytes 147464 | tf_op jit(solution)/shard_map/ppermute | solution.py:231

commit v5 on v4

--- a/solution.py
+++ b/solution.py
@@ -181,16 +181,16 @@
     first = rows[0, 0:21, :]
     second = rows[1, 0:HALF, :] + pltpu.roll(rows[1, HALF : 2 * HALF, :], 64, 1)
     value = jnp.concatenate([first, second], axis=0).astype(BF16)
-    for i in range(8):
+    for i in range(16):
         packed[i] = value
 
 
 def resum_kernel(got, out):
     total = got[0].astype(F32)
-    for i in range(1, 8):
+    for i in range(1, 16):
         total += got[i].astype(F32)
     total = total.astype(BF16)
-    for i in range(16):
+    for i in range(8):
         out[i] = total
 
 
@@ -212,7 +212,7 @@
 
 def last_kernel(got, gain_grad, tap_grad):
     value = got[0].astype(F32)
-    for i in range(1, 16):
+    for i in range(1, 8):
         value += got[i].astype(F32)
     value = value * SCALE
     tap_grad[:, :128] = value[0:TAPS]
@@ -271,18 +271,17 @@
     got = lax.all_gather(send, "chan")
     term, term16, packed = call(
         term_kernel,
-        (shape((CELLS, CH)), shape((CELLS, CH), BF16), shape((8, PACK, 128), BF16)),
+        (shape((CELLS, CH)), shape((CELLS, CH), BF16), shape((16, PACK, 128), BF16)),
         [SMEM] * 3 + [VMEM] * 4,
         (VMEM,) * 3,
         [pltpu.VMEM((2, 24, 128), F32)],
         "term",
     )(place, lon_offsets, basis, ext, fwd_t, gain_t, got)
-    one = lax.all_to_all(packed, "z", 0, 0)
-    term_far = swap_far(term)
-    one, term_again = lax.optimization_barrier((one, term16))
-    again = call(resum_kernel, shape((16, PACK, 128), BF16), [VMEM], VMEM, [], "resum")(one)
-    two = lax.all_to_all(again, ("y", "xh"), 0, 0)
-    term_near = swap_near(term_again)
+    one = lax.all_to_all(packed, ("y", "xh"), 0, 0)
+    term_far = swap_far(term16)
+    again = call(resum_kernel, shape((8, PACK, 128), BF16), [VMEM], VMEM, [], "resum")(one)
+    two = lax.all_to_all(again, "z", 0, 0)
+    term_near = swap_near(term)
     grad = call(
         adjoint_kernel,
         shape((CELLS, CH), BF16),
@@ -290,7 +289,7 @@
         VMEM,
         [pltpu.VMEM(ext_shape, F32), pltpu.VMEM((CELLS, CH), F32)],
         "adjoint",
-        flops=2_000_000_000,
+        flops=4000000000,
     )(place, lon_offsets, basis, term, term_near, term_far, taps, cot)
     gain_grad, tap_grad = call(
         last_kernel, (shape((1, CH)), shape((TAPS, CH))), [VMEM], (VMEM,) * 2, [], "last"

time: 70.5 us -> 70.9 us (level)
  waiting for transfers between devices: 3.66 us -> 5.54 us
  starting transfers between devices: 44.4 us -> 43.3 us
    all_to_all x2, waiting for transfers between devices: 1.33 us -> 5.28 us  [the longest x1 5.28 us: per_device(): two = lax.all_to_all(again, 'z', 0, 0)]
    ppermute x1, waiting for transfers between devices: 2.07 us -> 0.01 us  [swap_near(): return lax.ppermute(value, 'xh', [(0, 1), (1, 0)])]
    all_to_all x2, starting transfers between devices: 8.01 us -> 6.86 us  [the longest x1 3.51 us: per_device(): one = lax.all_to_all(packed, ('y', 'xh'), 0, 0)]
  transfers between devices with their start and end apart: 6 -> 6, of which waited for: 3 -> 2; matrix products, arithmetic and copies ran while one was open for 0% -> 0% of each run, Pallas kernels for 5% -> 5%
where the time goes in v5:
time: 70.9 us; the launch traced here: 70.3 us
  starting transfers between devices  43.3 us (61%)
  Pallas kernels  9.98 us (14%)
  blocking collectives  9.88 us (14%)
  waiting for transfers between devices  5.54 us (8%)
  between operations  0.83 us (1%)
  local copies, waits for them, and re-layouts  0.71 us (1%)
    ppermute x2, starting transfers between devices, swap_far(): lax.ppermute(value, GRID, [(i, (i + 1 if i % 2 else i - 1) % n) for i in...  21.6 us
    all_to_all x1, starting transfers between devices, per_device(): line = lax.all_to_all(slots, ('xh', 'chan'), 0, 0)  10.2 us
    all_gather x1, blocking collectives, per_device(): got = lax.all_gather(send, 'chan')  9.88 us
    all_to_all x1, waiting for transfers between devices, per_device(): two = lax.all_to_all(again, 'z', 0, 0)  5.28 us
    ppermute x1, starting transfers between devices, swap_near(): return lax.ppermute(value, 'xh', [(0, 1), (1, 0)])  4.65 us
    all_to_all x1, starting transfers between devices, per_device(): one = lax.all_to_all(packed, ('y', 'xh'), 0, 0)  3.51 us
    all_to_all x1, starting transfers between devices, per_device(): two = lax.all_to_all(again, 'z', 0, 0)  3.35 us
    pallas_call x1, Pallas kernels, per_device(): call(term_kernel, (shape((CELLS, CH)), shape((CELLS, CH), BF16), shape((1...  2.16 us
  transfers between devices with their start and end apart: 6, of which 2 were waited for; matrix products, arithmetic and copies ran while one was open for 0% of the time, Pallas kernels for 5%

profile of v5, /device:TPU:1, one launch (start us, length us, event | category | flops | bytes accessed | tf_op | source)
XLA Modules:
  0.0 70.3 jit_solution(3334714563701324790)
XLA Ops:
  0.6 0.0 copy-start.3
  0.6 0.0 copy-start.2
  0.7 0.0 copy-start.6
  0.7 0.0 copy-start
  0.7 0.0 copy-start.1
  0.7 1.9 %prep.1 = bf16[8,192,128]{2,1,0:T(8,128)(2,1)} custom-call(s32[1]{0:T(128)} %bitcast.place, bf16[128,192]{1,0:T(8,128)(2,1)} %bitcast.14, bf16[128,192]{1,0:T(8,128)(2,1)} %bitcast.10), custom_call_target="tpu_custom_call" | custom-call | flops 8000000000 | tf_op jit(solution)/shard_map/prep/pallas_call | solution.py:246
  2.6 10.2 %all-to-all-start = ((bf16[8,192,128]{2,1,0:T(8,128)(2,1)}), bf16[8,192,128]{2,1,0:T(8,128)(2,1)S(1)}, u32[]{:S(2)}, u32[]{:S(2)}) async-start(bf16[8,192,128]{2,1,0:T(8,128)(2,1)} %prep.1), calls=%async_computation | async-start | bytes 786432 | tf_op jit(solution)/shard_map/all_to_all | solution.py:249
  12.8 0.0 copy-done.3
  12.8 11.7 %collective-permute-start = (bf16[128,192]{1,0:T(8,128)(2,1)S(1)}, bf16[128,192]{1,0:T(8,128)(2,1)}, u32[]{:S(2)}, u32[]{:S(2)}) collective-permute-start(bf16[128,192]{1,0:T(8,128)(2,1)S(1)} %bitcast.11), channel_id=1, source_target_pairs={{0,508},{4,8},{8,4},{12,16},{16,12},{20,24},{24,20},{28,32},{32,28... | collective-permute-start | bytes 147464 | tf_op jit(solution)/shard_map/ppermute | solution.py:236
  24.6 0.0 copy-done.2
  24.6 0.0 copy-done.6
  24.6 0.0 copy-start.7
  24.6 0.7 copy-done.7
  25.3 0.2 ready.1
  25.5 0.0 all-to-all-done.line
  25.5 0.0 copy-done
  25.5 0.0 copy-done.1
  25.5 0.0 copy-start.4
  25.5 0.0 copy-start.5
  25.6 1.0 %mlp.1.part = bf16[768,128]{1,0:T(8,128)(2,1)S(1)} custom-call(s32[1]{0:T(128)} %bitcast.place, bf16[8,192,128]{2,1,0:T(8,128)(2,1)S(1)} %all-to-all-done.line, f32[128,768]{1,0:T(8,128)S(1)} %get-tuple-element.16.slope, bf16[768,768]{1,0:T(8,128)(2,1)S(1)} %copy-done, bf16[768,768]{1,0:T(8,128)(2,1)S(1)} %copy-done.1), custom_call_target="tpu_custom_call" | custom-call | flops 300000000 | tf_op jit(solution)/shard_map/mlp/pallas_call | solution.py:260
  26.6 0.3 collective-permute-done.far
  26.8 0.0 copy-done.4
  26.8 0.0 copy-done.5
  26.8 1.5 %forward.1 = (f32[192,128]{1,0:T(8,128)S(1)}, bf16[976,128]{1,0:T(8,128)(2,1)S(1)}, f32[2,384,128]{2,1,0:T(8,128)S(1)}) custom-call(s32[1]{0:T(128)} %bitcast.place, s32[16,20]{1,0:T(8,128)S(1)} %copy-done.4, f32[16,20]{1,0:T(8,128)S(1)} %copy-done.5, bf16[128,192]{1,0:T(8,128)(2,1)S(1)} %bitcast.12, bf16[8,192,128]{2,1,0:T(8,128)(2,1)S(1)} %all-to-all-done.line, ...), custom_call_target="tpu_custom_call" | custom-call | tf_op jit(solution)/shard_map/forward/pallas_call | solution.py:263
  28.3 9.9 %all-gather = bf16[3904,128]{1,0:T(8,128)(2,1)S(1)} all-gather(bf16[976,128]{1,0:T(8,128)(2,1)S(1)} %get-tuple-element.19), channel_id=2, replica_groups=mesh['z'=8,'y'=8,'xh'=2,'chan'=4] {'chan'}, dimensions={0}, use_global_device_ids=true | all-gather | bytes 1249280 | tf_op jit(solution)/shard_map/all_gather | solution.py:271
  38.2 0.0 copy-start.8
  38.2 2.2 %term.1 = (f32[128,192]{1,0:T(8,128)S(1)}, bf16[128,192]{1,0:T(8,128)(2,1)S(1)}, bf16[16,32,128]{2,1,0:T(8,128)(2,1)}) custom-call(s32[1]{0:T(128)} %bitcast.place, s32[16,20]{1,0:T(8,128)S(1)} %copy-done.4, f32[16,20]{1,0:T(8,128)S(1)} %copy-done.5, f32[2,384,128]{2,1,0:T(8,128)S(1)} %get-tuple-element.17.ext, f32[192,128]{1,0:T(8,128)S(1)} %get-tuple-element.18.fwd_t, ...), custom_call_target="tpu_custom_call" | custom-call | tf_op jit(solution)/shard_map/term/pallas_call | solution.py:272
  40.4 3.5 %all-to-all-start.1 = ((bf16[16,32,128]{2,1,0:T(8,128)(2,1)}), bf16[16,32,128]{2,1,0:T(8,128)(2,1)S(1)}, u32[]{:S(2)}, u32[]{:S(2)}) async-start(bf16[16,32,128]{2,1,0:T(8,128)(2,1)} %get-tuple-element.22), calls=%async_computation.1 | async-start | bytes 262144 | tf_op jit(solution)/shard_map/all_to_all | solution.py:280
  43.9 4.6 %collective-permute-start.1 = (f32[128,192]{1,0:T(8,128)S(1)}, f32[128,192]{1,0:T(8,128)S(1)}, u32[]{:S(2)}, u32[]{:S(2)}) collective-permute-start(f32[128,192]{1,0:T(8,128)S(1)} %get-tuple-element.20.own), channel_id=1, source_target_pairs={{0,4},{4,0},{1,5},{5,1},{2,6},{6,2},{3,7},{7,3},{8,12},{12,8},{9,1... | collective-permute-start | bytes 294920 | tf_op jit(solution)/shard_map/ppermute | solution.py:231
  48.5 9.9 %collective-permute-start.2 = (bf16[128,192]{1,0:T(8,128)(2,1)S(1)}, bf16[128,192]{1,0:T(8,128)(2,1)S(1)}, u32[]{:S(2)}, u32[]{:S(2)}) collective-permute-start(bf16[128,192]{1,0:T(8,128)(2,1)S(1)} %get-tuple-element.21), channel_id=1, source_target_pairs={{0,508},{4,8},{8,4},{12,16},{16,12},{20,24},{24,20},{28,32},{32,28... | collective-permute-start | bytes 147464 | tf_op jit(solution)/shard_map/ppermute | solution.py:236
  58.4 0.0 all-to-all-done.1.got
  58.4 0.6 resum.1
  59.1 3.3 %all-to-all-start.2 = ((bf16[8,32,128]{2,1,0:T(8,128)(2,1)}), bf16[8,32,128]{2,1,0:T(8,128)(2,1)S(1)}, u32[]{:S(2)}, u32[]{:S(2)}) async-start(bf16[8,32,128]{2,1,0:T(8,128)(2,1)} %resum.1), calls=%async_computation.2 | async-start | bytes 131072 | tf_op jit(solution)/shard_map/all_to_all | solution.py:283
  62.4 0.0 collective-permute-done.2.far
  62.4 0.0 collective-permute-done.1.near
  62.5 0.0 copy-done.8
  62.5 1.8 %adjoint.1 = bf16[128,192]{1,0:T(8,128)(2,1)} custom-call(s32[1]{0:T(128)} %bitcast.place, s32[16,20]{1,0:T(8,128)S(1)} %copy-done.4, f32[16,20]{1,0:T(8,128)S(1)} %copy-done.5, f32[128,192]{1,0:T(8,128)S(1)} %get-tuple-element.20.own, f32[128,192]{1,0:T(8,128)S(1)} %collective-permute-done.1.near, bf16[128,192]{1,0:T(8,128)(2,1)S(1)} %collective-permute-done.2.far, ...), custom_call_target="tpu_custom_call" | custom-call | flops 4000000000 | tf_op jit(solution)/shard_map/adjoint/pallas_call | solution.py:285
  64.3 5.3 %all-to-all-done.2.got = bf16[8,32,128]{2,1,0:T(8,128)(2,1)S(1)} async-done(((bf16[8,32,128]{2,1,0:T(8,128)(2,1)}), bf16[8,32,128]{2,1,0:T(8,128)(2,1)S(1)}, u32[]{:S(2)}, u32[]{:S(2)}) %all-to-all-start.2) | async-done | bytes 65568 | tf_op jit(solution)/shard_map/all_to_all | solution.py:283
  69.6 0.7 last.1
Async XLA Ops:
  0.6 12.2 %copy-start.3 = (bf16[16,8,192]{2,1,0:T(8,128)(2,1)S(1)}, bf16[16,8,192]{2,1,0:T(8,128)(2,1)}, u32[]{:S(2)}) copy-start(bf16[16,8,192]{2,1,0:T(8,128)(2,1)} %param.9) | copy-start | bytes 147460
  0.6 23.9 %copy-start.2 = (bf16[16,8,768]{2,1,0:T(8,128)(2,1)S(1)}, bf16[16,8,768]{2,1,0:T(8,128)(2,1)}, u32[]{:S(2)}) copy-start(bf16[16,8,768]{2,1,0:T(8,128)(2,1)} %param.11) | copy-start | bytes 589828
  0.7 23.9 %copy-start.6 = (f32[20,192]{1,0:T(8,128)S(1)}, f32[20,192]{1,0:T(8,128)}, u32[]{:S(2)}) copy-start(f32[20,192]{1,0:T(8,128)} %taps.1) | copy-start | bytes 46084
  0.7 24.8 %copy-start = (bf16[768,768]{1,0:T(8,128)(2,1)S(1)}, bf16[768,768]{1,0:T(8,128)(2,1)}, u32[]{:S(2)}) copy-start(bf16[768,768]{1,0:T(8,128)(2,1)} %down.1) | copy-start | bytes 3538948
  0.7 24.8 %copy-start.1 = (bf16[768,768]{1,0:T(8,128)(2,1)S(1)}, bf16[768,768]{1,0:T(8,128)(2,1)}, u32[]{:S(2)}) copy-start(bf16[768,768]{1,0:T(8,128)(2,1)} %up.1) | copy-start | bytes 3538948
  2.6 22.9 %all-to-all-start = ((bf16[8,192,128]{2,1,0:T(8,128)(2,1)}), bf16[8,192,128]{2,1,0:T(8,128)(2,1)S(1)}, u32[]{:S(2)}, u32[]{:S(2)}) async-start(bf16[8,192,128]{2,1,0:T(8,128)(2,1)} %prep.1), calls=%async_computation | async-start | bytes 786432 | tf_op jit(solution)/shard_map/all_to_all | solution.py:249
  12.8 14.0 %collective-permute-start = (bf16[128,192]{1,0:T(8,128)(2,1)S(1)}, bf16[128,192]{1,0:T(8,128)(2,1)}, u32[]{:S(2)}, u32[]{:S(2)}) collective-permute-start(bf16[128,192]{1,0:T(8,128)(2,1)S(1)} %bitcast.11), channel_id=1, source_target_pairs={{0,508},{4,8},{8,4},{12,16},{16,12},{20,24},{24,20},{28,32},{32,28... | collective-permute-start | bytes 147464 | tf_op jit(solution)/shard_map/ppermute | solution.py:236
  24.6 0.7 copy-start.7
  25.5 1.3 %copy-start.4 = (s32[16,20]{1,0:T(8,128)S(1)}, s32[16,20]{1,0:T(8,128)}, u32[]{:S(2)}) copy-start(s32[16,20]{1,0:T(8,128)} %offs.5) | copy-start | bytes 3844
  25.5 1.3 %copy-start.5 = (f32[16,20]{1,0:T(8,128)S(1)}, f32[16,20]{1,0:T(8,128)}, u32[]{:S(2)}) copy-start(f32[16,20]{1,0:T(8,128)} %basis.5) | copy-start | bytes 3844
  38.2 24.2 %copy-start.8 = (bf16[16,8,192]{2,1,0:T(8,128)(2,1)S(1)}, bf16[16,8,192]{2,1,0:T(8,128)(2,1)}, u32[]{:S(2)}) copy-start(bf16[16,8,192]{2,1,0:T(8,128)(2,1)} %param.10) | copy-start | bytes 147460
  40.4 18.0 %all-to-all-start.1 = ((bf16[16,32,128]{2,1,0:T(8,128)(2,1)}), bf16[16,32,128]{2,1,0:T(8,128)(2,1)S(1)}, u32[]{:S(2)}, u32[]{:S(2)}) async-start(bf16[16,32,128]{2,1,0:T(8,128)(2,1)} %get-tuple-element.22), calls=%async_computation.1 | async-start | bytes 262144 | tf_op jit(solution)/shard_map/all_to_all | solution.py:280
  43.9 18.6 %collective-permute-start.1 = (f32[128,192]{1,0:T(8,128)S(1)}, f32[128,192]{1,0:T(8,128)S(1)}, u32[]{:S(2)}, u32[]{:S(2)}) collective-permute-start(f32[128,192]{1,0:T(8,128)S(1)} %get-tuple-element.20.own), channel_id=1, source_target_pairs={{0,4},{4,0},{1,5},{5,1},{2,6},{6,2},{3,7},{7,3},{8,12},{12,8},{9,1... | collective-permute-start | bytes 294920 | tf_op jit(solution)/shard_map/ppermute | solution.py:231
  48.5 13.9 %collective-permute-start.2 = (bf16[128,192]{1,0:T(8,128)(2,1)S(1)}, bf16[128,192]{1,0:T(8,128)(2,1)S(1)}, u32[]{:S(2)}, u32[]{:S(2)}) collective-permute-start(bf16[128,192]{1,0:T(8,128)(2,1)S(1)} %get-tuple-element.21), channel_id=1, source_target_pairs={{0,508},{4,8},{8,4},{12,16},{16,12},{20,24},{24,20},{28,32},{32,28... | collective-permute-start | bytes 147464 | tf_op jit(solution)/shard_map/ppermute | solution.py:236
  59.1 10.5 %all-to-all-start.2 = ((bf16[8,32,128]{2,1,0:T(8,128)(2,1)}), bf16[8,32,128]{2,1,0:T(8,128)(2,1)S(1)}, u32[]{:S(2)}, u32[]{:S(2)}) async-start(bf16[8,32,128]{2,1,0:T(8,128)(2,1)} %resum.1), calls=%async_computation.2 | async-start | bytes 131072 | tf_op jit(solution)/shard_map/all_to_all | solution.py:283
